TPU v7x, 32 devices: a whole 2x2x4 slice. The times are simulated.
32 devices in a mesh: outer: 8 (over y, x, core), inner: 4 (over z).
Axes of the slice: x: 2, y: 2, z: 4, core: 2. Of those that a mesh axis runs over, the one named last changes fastest.
Arguments:
- projected: bfloat16 [4096, 12288], P(('outer', 'inner')), may hold values from -6 to 6
- short_taps: float32 [3, 12288], replicated, may hold values from -3 to 3
- rates: float32 [4096, 16], replicated, may hold values from 6.1035156e-05 to 0.05
- residues: float32 [4096, 16], replicated, may hold values from -1.5 to 1.5
- skip_gain: float32 [4096], replicated, may hold values from -4 to 4
Outputs:
- gated: bfloat16 [4096, 4096], P(('outer', 'inner'))
All inputs are finite; a program needn't handle non-finite values.
Results may differ from a plain program's by a relative error of at most 0.008.
Values may be sent and summed in bfloat16 or wider, within the bound.
No kernel may reach another device: no remote copies, remote signals or barrier semaphores. Data moves between devices by JAX's collectives and lax.ppermute only.
A program may use at most 128 MiB of HBM per device.

v0:
```python
import jax
import jax.numpy as jnp
from jax import lax
from jax.sharding import PartitionSpec as P

HIGH = lax.Precision.HIGHEST
TWO_PI = 2.0 * 3.141592653589793


def passed_along(value, axis, steps):
    count = lax.axis_size(axis)
    leading, last = (max(0, -steps), min(count, count - steps))
    return lax.ppermute(value, axis, [(source, source + steps) for source in range(leading, last)])


def phase_table(count_rows, count_cols, modulus, sign):
    product = (
        jnp.arange(count_rows, dtype=jnp.int32)[:, None]
        * jnp.arange(count_cols, dtype=jnp.int32)[None, :]
        % modulus
    )
    angle = sign * TWO_PI / modulus * product.astype(jnp.float32)
    return (jnp.cos(angle), jnp.sin(angle))


def complex_times(left_re, left_im, right_re, right_im):
    return (left_re * right_re - left_im * right_im, left_re * right_im + left_im * right_re)


def middle_segment(
    sec_re, sec_im, k_values, ko_count, inner_count, rows, rates, residues, chan_start, chan_local
):
    full_blocks = ko_count * inner_count
    length = full_blocks * rows
    tokens_total = length // 2
    inner_re, inner_im = phase_table(inner_count, inner_count, inner_count, -1.0)
    mid_re = jnp.einsum("ji,ckis->ckjs", inner_re, sec_re, precision=HIGH) - jnp.einsum(
        "ji,ckis->ckjs", inner_im, sec_im, precision=HIGH
    )
    mid_im = jnp.einsum("ji,ckis->ckjs", inner_re, sec_im, precision=HIGH) + jnp.einsum(
        "ji,ckis->ckjs", inner_im, sec_re, precision=HIGH
    )
    block_freq = k_values[:, None] + ko_count * jnp.arange(inner_count, dtype=jnp.int32)[None, :]
    spots = jnp.arange(rows, dtype=jnp.int32)
    twist = (
        -TWO_PI
        / length
        * (block_freq[:, :, None] * spots[None, None, :] % length).astype(jnp.float32)
    )
    twist_re = jnp.cos(twist)[None]
    twist_im = jnp.sin(twist)[None]
    mid_re, mid_im = complex_times(mid_re, mid_im, twist_re, twist_im)
    local_re, local_im = phase_table(rows, rows, rows, -1.0)
    spec_re = jnp.einsum("ckjs,sq->ckjq", mid_re, local_re, precision=HIGH) - jnp.einsum(
        "ckjs,sq->ckjq", mid_im, local_im, precision=HIGH
    )
    spec_im = jnp.einsum("ckjs,sq->ckjq", mid_re, local_im, precision=HIGH) + jnp.einsum(
        "ckjs,sq->ckjq", mid_im, local_re, precision=HIGH
    )
    freq = block_freq[:, :, None] + full_blocks * jnp.arange(rows, dtype=jnp.int32)[None, None, :]
    angle = -TWO_PI / length * freq.astype(jnp.float32)
    half_sine = jnp.sin(0.5 * angle)[None]
    full_sine = jnp.sin(angle)[None]
    parity = (1 - 2 * (freq % 2)).astype(jnp.float32)[None]
    my_rates = lax.dynamic_slice_in_dim(rates, chan_start, chan_local, 0)
    my_residues = lax.dynamic_slice_in_dim(residues, chan_start, chan_local, 0)
    filter_re = jnp.zeros(spec_re.shape, jnp.float32)
    filter_im = jnp.zeros(spec_re.shape, jnp.float32)
    for mode in range(rates.shape[1]):
        rate = my_rates[:, mode][:, None, None, None]
        decay = jnp.exp(-rate)
        amplitude = my_residues[:, mode][:, None, None, None] * jnp.sqrt(2.0 * rate)
        numer = amplitude * (1.0 - jnp.exp(-rate * tokens_total) * parity)
        denom_re = -jnp.expm1(-rate) + 2.0 * decay * half_sine * half_sine
        denom_im = -decay * full_sine
        magnitude = denom_re * denom_re + denom_im * denom_im
        filter_re = filter_re + numer * denom_re / magnitude
        filter_im = filter_im - numer * denom_im / magnitude
    prod_re, prod_im = complex_times(spec_re, spec_im, filter_re, filter_im)
    back_re = jnp.einsum("ckjq,sq->ckjs", prod_re, local_re, precision=HIGH) + jnp.einsum(
        "ckjq,sq->ckjs", prod_im, local_im, precision=HIGH
    )
    back_im = jnp.einsum("ckjq,sq->ckjs", prod_im, local_re, precision=HIGH) - jnp.einsum(
        "ckjq,sq->ckjs", prod_re, local_im, precision=HIGH
    )
    back_re, back_im = complex_times(back_re, back_im, twist_re, -twist_im)
    undo_re = jnp.einsum("ji,ckjs->ckis", inner_re, back_re, precision=HIGH) + jnp.einsum(
        "ji,ckjs->ckis", inner_im, back_im, precision=HIGH
    )
    undo_im = jnp.einsum("ji,ckjs->ckis", inner_re, back_im, precision=HIGH) - jnp.einsum(
        "ji,ckjs->ckis", inner_im, back_re, precision=HIGH
    )
    return (undo_re, undo_im)


def on_device(projected, short_taps, rates, residues, skip_gain):
    rows = projected.shape[0]
    feature_width = projected.shape[1]
    channels = feature_width // 3
    outer_count = lax.axis_size("outer")
    inner_count = lax.axis_size("inner")
    outer_place = lax.axis_index("outer")
    inner_place = lax.axis_index("inner")
    previous = passed_along(projected[rows - 2 :], ("outer", "inner"), 1)
    padded = jnp.concatenate([previous, projected], 0).astype(jnp.float32)
    feat = short_taps[0] * padded[2:] + short_taps[1] * padded[1:-1] + short_taps[2] * padded[:-2]
    query = feat[:, :channels]
    mixed = feat[:, channels : 2 * channels] * feat[:, 2 * channels :]
    segmented = mixed.T
    ko_count = 2 * outer_count
    full_blocks = ko_count * inner_count
    length = full_blocks * rows
    chan_local = channels // (outer_count * inner_count)
    chan_start = (outer_place * inner_count + inner_place) * chan_local
    sections = segmented.reshape(outer_count, inner_count, chan_local, 1, 1, rows)
    gathered = lax.all_to_all(
        lax.all_to_all(
            sections.astype(jnp.bfloat16), "outer", split_axis=0, concat_axis=3, tiled=True
        ),
        "inner",
        split_axis=1,
        concat_axis=4,
        tiled=True,
    ).astype(sections.dtype)
    signal = gathered.reshape(chan_local, outer_count, inner_count, rows)
    i_values = jnp.arange(inner_count, dtype=jnp.int32)
    outer_re, outer_im = phase_table(ko_count, outer_count, ko_count, -1.0)
    spin_re = jnp.einsum("ko,cois->ckis", outer_re, signal, precision=HIGH)
    spin_im = jnp.einsum("ko,cois->ckis", outer_im, signal, precision=HIGH)
    ko_axis = jnp.arange(ko_count, dtype=jnp.int32)
    turn = (
        -TWO_PI
        / full_blocks
        * (ko_axis[:, None] * i_values[None, :] % full_blocks).astype(jnp.float32)
    )
    first_re = jnp.cos(turn)[None, :, :, None]
    first_im = jnp.sin(turn)[None, :, :, None]
    spin_re, spin_im = complex_times(spin_re, spin_im, first_re, first_im)
    undo_re, undo_im = middle_segment(
        spin_re,
        spin_im,
        ko_axis,
        ko_count,
        inner_count,
        rows,
        rates,
        residues,
        chan_start,
        chan_local,
    )
    home_re, home_im = (undo_re, undo_im)
    home_re, home_im = complex_times(home_re, home_im, first_re, -first_im)
    real_part = jnp.einsum("ko,ckis->cois", outer_re, home_re, precision=HIGH) + jnp.einsum(
        "ko,ckis->cois", outer_im, home_im, precision=HIGH
    )
    real_part = real_part * (1.0 / length)
    arranged = real_part.reshape(1, 1, chan_local, outer_count, inner_count, rows)
    settled = lax.all_to_all(
        lax.all_to_all(
            arranged.astype(jnp.bfloat16), "outer", split_axis=3, concat_axis=0, tiled=True
        ),
        "inner",
        split_axis=4,
        concat_axis=1,
        tiled=True,
    ).astype(arranged.dtype)
    conv = settled.reshape(channels, rows).T
    return (query * (conv + skip_gain[None, :] * mixed)).astype(jnp.bfloat16)


def solution(mesh):
    in_specs = (P(("outer", "inner"), None), P(), P(), P(), P())
    out_specs = P(("outer", "inner"), None)
    return jax.shard_map(
        on_device, mesh=mesh, in_specs=in_specs, out_specs=out_specs, check_vma=False
    )
```

profile of v0, /device:TPU:0, one launch (start us, length us, event | category | flops | bytes accessed | tf_op | source)
XLA Modules:
  0.0 313.8 jit_solution(15967212766667482407)
XLA Ops:
  0.0 1.0 slice.127
  1.0 4.9 %collective-permute-start = (bf16[2,12288]{1,0:T(2,128)(2,1)S(1)}, bf16[2,12288]{1,0:T(2,128)(2,1)S(1)}, u32[]{:S(2)}, u32[]{:S(2)}) collective-permute-start(bf16[2,12288]{1,0:T(2,128)(2,1)S(1)} %slice.127), channel_id=1, source_target_pairs={{0,1},{1,2},{2,3},{3,4},{4,5},{5,6},{6,7},{7,8},{8,9},{9,10},{10,1... | collective-permute-start | bytes 147464 | tf_op jit(solution)/shard_map/ppermute | solution.py:13
  5.9 0.1 fusion.183
  6.0 0.3 fusion.112.clone.4
  6.2 0.1 fusion.185
  6.3 1.3 fusion.285
  7.6 2.1 exponential_bitcast_fusion.15
  9.7 3.5 %copy.52 = bf16[128,12288]{0,1:T(8,128)(2,1)S(1)} copy(bf16[128,12288]{1,0:T(8,128)(2,1)} %param.5) | data formatting | bytes 6291456 | tf_op args[0]
  13.2 0.0 collective-permute-done
  13.2 2.8 copy.51
  16.0 4.0 %maximum_convert_fusion = f32[130,12288]{0,1:T(8,128)S(1)} fusion(bf16[128,12288]{0,1:T(8,128)(2,1)S(1)} %copy.52, bf16[2,12288]{0,1:T(8,128)(2,1)} %copy.51), kind=kLoop, calls=%fused_computation.5 | loop fusion | flops 6389760 | bytes 9584640 | tf_op jit(solution)/shard_map/convert_element_type | solution.py:105
  20.0 9.5 %fusion = f32[128,12288]{0,1:T(8,128)S(1)} fusion(f32[130,12288]{0,1:T(8,128)S(1)} %maximum_convert_fusion, f32[12288]{0:T(1024)S(1)} %bitcast.322, f32[12288]{0:T(1024)S(1)} %bitcast.323, f32[12288]{0:T(1024)S(1)} %bitcast.321), kind=kLoop, calls=%fused_computation.1 | loop fusion | flops 7864320 | bytes 25313280 | tf_op jit(solution)/shard_map/add | solution.py:106
  29.6 0.0 copy-start
  29.6 2.7 copy-done
  32.3 0.2 fusion.98
  32.5 1.8 copy.53
  34.3 3.7 %all-to-all-start = ((bf16[8,4,128,1,1,128]{5,1,2,4,3,0:T(4,128)(2,1)}), bf16[8,4,128,1,1,128]{5,1,2,4,3,0:T(4,128)(2,1)S(1)}, u32[]{:S(2)}, u32[]{:S(2)}) async-start(bf16[8,4,128,1,1,128]{5,1,2,4,3,0:T(4,128)(2,1)} %copy.53), calls=%async_computation | async-start | bytes 2097152 | tf_op jit(solution)/shard_map/all_to_all | solution.py:117
  38.0 0.7 copy.73
  38.7 0.7 copy.72
  39.4 14.0 %all-to-all-done = bf16[8,4,128,1,1,128]{5,1,2,4,3,0:T(4,128)(2,1)S(1)} async-done(((bf16[8,4,128,1,1,128]{5,1,2,4,3,0:T(4,128)(2,1)}), bf16[8,4,128,1,1,128]{5,1,2,4,3,0:T(4,128)(2,1)S(1)}, u32[]{:S(2)}, u32[]{:S(2)}) %all-to-all-start) | async-done | bytes 1048608 | tf_op jit(solution)/shard_map/all_to_all | solution.py:117
  53.4 1.6 copy.54
  55.1 4.4 %all-to-all-start.1 = ((bf16[1,4,128,8,1,128]{5,3,2,4,0,1:T(8,128)(2,1)}), bf16[1,4,128,8,1,128]{5,3,2,4,0,1:T(8,128)(2,1)S(1)}, u32[]{:S(2)}, u32[]{:S(2)}) async-start(bf16[1,4,128,8,1,128]{5,3,2,4,0,1:T(8,128)(2,1)} %copy.54), calls=%async_computation.1 | async-start | bytes 2097152 | tf_op jit(solution)/shard_map/all_to_all | solution.py:116
  59.6 0.1 fusion.126
  59.7 1.4 fusion.120
  61.0 21.3 %all-to-all-done.1 = bf16[1,4,128,8,1,128]{5,3,2,4,0,1:T(8,128)(2,1)S(1)} async-done(((bf16[1,4,128,8,1,128]{5,3,2,4,0,1:T(8,128)(2,1)}), bf16[1,4,128,8,1,128]{5,3,2,4,0,1:T(8,128)(2,1)S(1)}, u32[]{:S(2)}, u32[]{:S(2)}) %all-to-all-start.1) | async-done | bytes 1048608 | tf_op jit(solution)/shard_map/all_to_all | solution.py:116
  82.4 1.9 fusion.94
  84.3 2.6 fusion.52
  86.9 8.0 %fusion.68 = f32[128,16,128,4]{2,3,1,0:T(4,128)S(1)} fusion(f32[128,16,4,128]{3,1,2,0:T(8,128)S(1)} %get-tuple-element.47), kind=kOutput, calls=%fused_computation.153 | convolution fusion | flops 50331872 | bytes 8388608 | tf_op jit(solution)/shard_map/ji,ckis->ckjs/dot_general | solution.py:37
  94.8 8.1 %fusion.66 = f32[128,16,128,4]{2,3,1,0:T(4,128)S(1)} fusion(f32[128,16,4,128]{3,1,2,0:T(8,128)S(1)} %get-tuple-element.47), kind=kOutput, calls=%fused_computation.151 | convolution fusion | flops 50331872 | bytes 8388608 | tf_op jit(solution)/shard_map/ji,ckis->ckjs/dot_general | solution.py:40
  103.0 8.7 %fusion.74 = f32[128,16,128,4]{2,3,1,0:T(4,128)S(1)} fusion(f32[128,16,128,4]{2,3,1,0:T(4,128)S(1)} %fusion.68, f32[128,16,4,128]{3,1,2,0:T(8,128)S(1)} %get-tuple-element.46), kind=kOutput, calls=%fused_computation.159 | convolution fusion | flops 51380448 | bytes 12582912 | tf_op jit(solution)/shard_map/ji,ckis->ckjs/dot_general | solution.py:37
  111.6 0.0 copy-done.2
  111.6 10.3 %fusion.50 = (f32[128,16,4,128]{3,2,1,0:T(4,128)S(1)}, f32[128,16,4,128]{3,2,1,0:T(4,128)S(1)}) fusion(f32[128,16,128,4]{2,3,1,0:T(4,128)S(1)} %fusion.74, f32[16,4,128]{2,1,0:T(4,128)S(1)} %get-tuple-element.115, f32[16,4,128]{2,1,0:T(4,128)S(1)} %get-tuple-element.116, f32[128,16,128,4]{2,3,1,0:T(4,128)S(1)} %fusion.66, ...), kind=kOutput, calls=%fused_computation.88 | convolution fusion | flops 57671904 | bytes 21037056 | tf_op jit(solution)/shard_map/ji,ckis->ckjs/dot_general | solution.py:40
  122.0 6.8 %fusion.60 = f32[128,16,4,128]{3,0,2,1:T(8,128)S(1)} fusion(f32[128,16,4,128]{3,2,1,0:T(4,128)S(1)} %get-tuple-element.43), kind=kOutput, calls=%fused_computation.145 | convolution fusion | flops 1610842112 | bytes 8388608 | tf_op jit(solution)/shard_map/ckjs,sq->ckjq/dot_general | solution.py:54
  128.8 7.2 %fusion.58 = f32[128,16,4,128]{3,0,2,1:T(8,128)S(1)} fusion(f32[128,16,4,128]{3,2,1,0:T(4,128)S(1)} %get-tuple-element.43), kind=kOutput, calls=%fused_computation.143 | convolution fusion | flops 1610842112 | bytes 8388608 | tf_op jit(solution)/shard_map/ckjs,sq->ckjq/dot_general | solution.py:57
  136.0 0.0 copy-start.8
  136.2 6.8 %fusion.80 = f32[128,16,4,128]{3,0,2,1:T(8,128)S(1)} fusion(f32[128,16,4,128]{3,0,2,1:T(8,128)S(1)} %fusion.60, f32[128,16,4,128]{3,2,1,0:T(4,128)S(1)} %get-tuple-element.42), kind=kOutput, calls=%fused_computation.161 | convolution fusion | flops 1611890688 | bytes 12582912 | tf_op jit(solution)/shard_map/ckjs,sq->ckjq/dot_general | solution.py:54
  143.1 44.3 %multiply_subtract_fusion.1 = (f32[128,16,4,128]{3,0,2,1:T(8,128)S(1)}, f32[128,16,4,128]{3,0,2,1:T(8,128)}, f32[128,16,4,128]{3,0,2,1:T(8,128)}, f32[128,16,4,128]{3,0,2,1:T(8,128)}) fusion(f32[128,16,4,128]{3,0,2,1:T(8,128)S(1)} %fusion.80, f32[128]{0:T(128)S(1)} %get-tuple-element.177, f32[128]{0:T(128)S(1)} %get-tuple-element.179, ...), kind=kOutput, calls=%fused_computation.109 | convolution fusion | flops 1882193920 | bytes 29564928 | tf_op jit(solution)/shard_map/ckjs,sq->ckjq/dot_general | solution.py:57
  187.5 3.7 %fusion.104 = f32[128,16,4,128]{3,0,2,1:T(8,128)S(1)} fusion(f32[128,16,4,128]{3,0,2,1:T(8,128)S(1)} %get-tuple-element.5), kind=kOutput, calls=%fused_computation.191 | convolution fusion | flops 1610842112 | bytes 8388608 | tf_op jit(solution)/shard_map/ckjq,sq->ckjs/dot_general | solution.py:80
  191.1 5.7 %fusion.108 = f32[128,16,4,128]{3,0,2,1:T(8,128)} fusion(f32[128,16,4,128]{3,0,2,1:T(8,128)S(1)} %get-tuple-element.5), kind=kOutput, calls=%fused_computation.195 | convolution fusion | flops 1610842112 | bytes 8388608 | tf_op jit(solution)/shard_map/ckjq,sq->ckjs/dot_general | solution.py:83
  196.8 6.6 %multiply_add_fusion.1 = f32[128,16,4,128]{3,0,2,1:T(8,128)S(1)} fusion(f32[128,16,4,128]{3,0,2,1:T(8,128)} %get-tuple-element.180, f32[128,16,4,128]{3,0,2,1:T(8,128)} %get-tuple-element.7, f32[128,16,4,128]{3,0,2,1:T(8,128)S(1)} %fusion.80, f32[128,16,4,128]{3,0,2,1:T(8,128)} %get-tuple-element.6), kind=kLoop, calls=%fused_computation.108 | loop fusion | flops 3145728 | bytes 20971520 | tf_op jit(solution)/shard_map/add | solution.py:27
  203.4 3.7 %fusion.110 = f32[128,16,4,128]{3,0,2,1:T(8,128)S(1)} fusion(f32[128,16,4,128]{3,0,2,1:T(8,128)S(1)} %multiply_add_fusion.1), kind=kOutput, calls=%fused_computation.197 | convolution fusion | flops 1610842112 | bytes 8388608 | tf_op jit(solution)/shard_map/ckjq,sq->ckjs/dot_general | solution.py:80
  207.1 5.5 %fusion.102 = f32[128,16,4,128]{3,0,2,1:T(8,128)} fusion(f32[128,16,4,128]{3,0,2,1:T(8,128)S(1)} %multiply_add_fusion.1), kind=kOutput, calls=%fused_computation.189 | convolution fusion | flops 1610842112 | bytes 8388608 | tf_op jit(solution)/shard_map/ckjq,sq->ckjs/dot_general | solution.py:83
  212.6 0.0 copy-done.3
  212.6 11.3 %multiply_subtract_fusion = (f32[128,16,4,128]{3,2,1,0:T(4,128)S(1)}, f32[128,16,4,128]{3,2,1,0:T(4,128)S(1)}) fusion(f32[16,4,128]{2,1,0:T(4,128)S(1)} %copy-done.4, f32[16,4,128]{2,1,0:T(4,128)S(1)} %copy-done.3, f32[128,16,4,128]{3,0,2,1:T(8,128)S(1)} %fusion.110, f32[128,16,4,128]{3,0,2,1:T(8,128)S(1)} %fusion.104, ...), kind=kLoop, calls=%fused_computation.107 | loop fusion | flops 8388608 | bytes 25231360 | tf_op jit(solution)/shard_map/sub | solution.py:27
  223.9 7.5 %fusion.161 = f32[128,16,128,4]{2,3,1,0:T(4,128)S(1)} fusion(f32[128,16,4,128]{3,2,1,0:T(4,128)S(1)} %get-tuple-element.41), kind=kOutput, calls=%fused_computation.255 | convolution fusion | flops 50331872 | bytes 8388608 | tf_op jit(solution)/shard_map/ji,ckjs->ckis/dot_general | solution.py:90
  231.4 7.7 %fusion.163 = f32[128,16,128,4]{2,3,1,0:T(4,128)S(1)} fusion(f32[128,16,4,128]{3,2,1,0:T(4,128)S(1)} %get-tuple-element.40), kind=kOutput, calls=%fused_computation.257 | convolution fusion | flops 50331872 | bytes 8388608 | tf_op jit(solution)/shard_map/ji,ckjs->ckis/dot_general | solution.py:87
  239.1 0.0 copy-start.5
  239.2 0.0 copy-start.6
  239.2 8.1 %convolution_subtract_fusion = f32[128,16,128,4]{2,3,1,0:T(4,128)S(1)} fusion(f32[128,16,128,4]{2,3,1,0:T(4,128)S(1)} %fusion.161, f32[128,16,4,128]{3,2,1,0:T(4,128)S(1)} %get-tuple-element.40), kind=kOutput, calls=%fused_computation.163 | convolution fusion | flops 51380448 | bytes 12582912 | tf_op jit(solution)/shard_map/ji,ckjs->ckis/dot_general | solution.py:90
  247.3 9.7 %subtract_bitcast_fusion = (f32[128,16,4,128]{3,2,1,0:T(4,128)S(1)}, f32[128,16,4,128]{3,2,1,0:T(4,128)S(1)}) fusion(f32[128,16,128,4]{2,3,1,0:T(4,128)S(1)} %convolution_subtract_fusion, f32[16,4]{1,0:T(8,128)S(1)} %copy-done.5, f32[16,4]{1,0:T(8,128)S(1)} %copy-done.6, f32[128,16,128,4]{2,3,1,0:T(4,128)S(1)} %fusion.163, ...), kind=kOutput, calls=%fused_computation.105 | convolution fusion | flops 57671904 | bytes 20972032 | tf_op jit(solution)/shard_map/ji,ckjs->ckis/dot_general | solution.py:87
  257.0 2.3 fusion.54
  259.4 0.0 slice-start
  259.4 2.5 fusion.89
  261.8 0.4 copy.76
  262.3 0.0 slice-start.1
  262.3 20.2 %all_to_all.60 = bf16[1,1,128,8,4,128]{5,4,2,1,0,3:T(4,128)(2,1)S(1)} all-to-all(bf16[1,1,128,8,4,128]{5,4,2,1,0,3:T(4,128)(2,1)S(1)} %copy.76), channel_id=1, replica_groups=mesh['outer'=8,'inner'=4] {'outer'}, dimensions={3} | all-to-all | bytes 2097152 | tf_op jit(solution)/shard_map/all_to_all | solution.py:159
  282.5 0.7 copy.77
  283.2 27.8 %all_to_all.61 = bf16[8,1,128,1,4,128]{5,0,2,3,1,4:T(8,128)(2,1)S(1)} all-to-all(bf16[8,1,128,1,4,128]{5,0,2,3,1,4:T(8,128)(2,1)S(1)} %copy.77), channel_id=1, replica_groups=mesh['outer'=8,'inner'=4] {'inner'}, dimensions={4} | all-to-all | bytes 2097152 | tf_op jit(solution)/shard_map/all_to_all | solution.py:158
  310.9 0.2 bitcast_convert_fusion
  311.2 0.0 slice-done
  311.2 0.0 slice-done.1
  311.2 0.0 copy-done.7
  311.2 1.1 fusion.86
  312.3 1.3 copy.79
  (46 shorter events, 0.2 us)
Async XLA Ops:
  1.0 12.2 %collective-permute-start = (bf16[2,12288]{1,0:T(2,128)(2,1)S(1)}, bf16[2,12288]{1,0:T(2,128)(2,1)S(1)}, u32[]{:S(2)}, u32[]{:S(2)}) collective-permute-start(bf16[2,12288]{1,0:T(2,128)(2,1)S(1)} %slice.127), channel_id=1, source_target_pairs={{0,1},{1,2},{2,3},{3,4},{4,5},{5,6},{6,7},{7,8},{8,9},{9,10},{10,1... | collective-permute-start | bytes 147464 | tf_op jit(solution)/shard_map/ppermute | solution.py:13
  29.6 2.7 copy-start
  34.3 19.1 %all-to-all-start = ((bf16[8,4,128,1,1,128]{5,1,2,4,3,0:T(4,128)(2,1)}), bf16[8,4,128,1,1,128]{5,1,2,4,3,0:T(4,128)(2,1)S(1)}, u32[]{:S(2)}, u32[]{:S(2)}) async-start(bf16[8,4,128,1,1,128]{5,1,2,4,3,0:T(4,128)(2,1)} %copy.53), calls=%async_computation | async-start | bytes 2097152 | tf_op jit(solution)/shard_map/all_to_all | solution.py:117
  55.1 27.3 %all-to-all-start.1 = ((bf16[1,4,128,8,1,128]{5,3,2,4,0,1:T(8,128)(2,1)}), bf16[1,4,128,8,1,128]{5,3,2,4,0,1:T(8,128)(2,1)S(1)}, u32[]{:S(2)}, u32[]{:S(2)}) async-start(bf16[1,4,128,8,1,128]{5,3,2,4,0,1:T(8,128)(2,1)} %copy.54), calls=%async_computation.1 | async-start | bytes 2097152 | tf_op jit(solution)/shard_map/all_to_all | solution.py:116
  61.0 50.6 %copy-start.2 = (f32[16,4,128]{2,1,0:T(4,128)}, f32[16,4,128]{2,1,0:T(4,128)S(1)}, u32[]{:S(2)}) copy-start(f32[16,4,128]{2,1,0:T(4,128)S(1)} %get-tuple-element.116) | copy-start | bytes 98308
  136.0 7.0 %copy-start.8 = (f32[128]{0:T(128)S(1)}, f32[128]{0:T(128)}, u32[]{:S(2)}) copy-start(f32[128]{0:T(128)} %get-tuple-element.84) | copy-start | bytes 1540
  136.1 7.0 %copy-start.9 = (f32[128]{0:T(128)S(1)}, f32[128]{0:T(128)}, u32[]{:S(2)}) copy-start(f32[128]{0:T(128)} %get-tuple-element.86) | copy-start | bytes 1540
  136.1 7.0 %copy-start.10 = (f32[128]{0:T(128)S(1)}, f32[128]{0:T(128)}, u32[]{:S(2)}) copy-start(f32[128]{0:T(128)} %get-tuple-element.88) | copy-start | bytes 1540
  136.1 7.0 %copy-start.11 = (f32[128]{0:T(128)S(1)}, f32[128]{0:T(128)}, u32[]{:S(2)}) copy-start(f32[128]{0:T(128)} %get-tuple-element.90) | copy-start | bytes 1540
  136.1 7.0 %copy-start.12 = (f32[128]{0:T(128)S(1)}, f32[128]{0:T(128)}, u32[]{:S(2)}) copy-start(f32[128]{0:T(128)} %get-tuple-element.92) | copy-start | bytes 1540
  136.1 7.0 %copy-start.13 = (f32[128]{0:T(128)S(1)}, f32[128]{0:T(128)}, u32[]{:S(2)}) copy-start(f32[128]{0:T(128)} %get-tuple-element.94) | copy-start | bytes 1540
  136.1 7.0 %copy-start.14 = (f32[128]{0:T(128)S(1)}, f32[128]{0:T(128)}, u32[]{:S(2)}) copy-start(f32[128]{0:T(128)} %get-tuple-element.96) | copy-start | bytes 1540
  136.1 7.0 %copy-start.15 = (f32[128]{0:T(128)S(1)}, f32[128]{0:T(128)}, u32[]{:S(2)}) copy-start(f32[128]{0:T(128)} %get-tuple-element.98) | copy-start | bytes 1540
  136.1 7.0 %copy-start.16 = (f32[128]{0:T(128)S(1)}, f32[128]{0:T(128)}, u32[]{:S(2)}) copy-start(f32[128]{0:T(128)} %get-tuple-element.100) | copy-start | bytes 1540
  136.1 7.0 %copy-start.17 = (f32[128]{0:T(128)S(1)}, f32[128]{0:T(128)}, u32[]{:S(2)}) copy-start(f32[128]{0:T(128)} %get-tuple-element.102) | copy-start | bytes 1540
  136.1 7.0 %copy-start.18 = (f32[128]{0:T(128)S(1)}, f32[128]{0:T(128)}, u32[]{:S(2)}) copy-start(f32[128]{0:T(128)} %get-tuple-element.104) | copy-start | bytes 1540
  136.2 7.0 %copy-start.19 = (f32[128]{0:T(128)S(1)}, f32[128]{0:T(128)}, u32[]{:S(2)}) copy-start(f32[128]{0:T(128)} %get-tuple-element.106) | copy-start | bytes 1540
  136.2 7.0 %copy-start.20 = (f32[128]{0:T(128)S(1)}, f32[128]{0:T(128)}, u32[]{:S(2)}) copy-start(f32[128]{0:T(128)} %get-tuple-element.107) | copy-start | bytes 1540
  207.1 5.5 %copy-start.1 = (f32[128,16,4,128]{3,0,2,1:T(8,128)S(1)}, f32[128,16,4,128]{3,0,2,1:T(8,128)}, u32[]{:S(2)}) copy-start(f32[128,16,4,128]{3,0,2,1:T(8,128)} %fusion.108) | copy-start | bytes 12582916
  207.1 5.5 %copy-start.3 = (f32[16,4,128]{2,1,0:T(4,128)S(1)}, f32[16,4,128]{2,1,0:T(4,128)}, u32[]{:S(2)}) copy-start(f32[16,4,128]{2,1,0:T(4,128)} %copy-done.2) | copy-start | bytes 98308
  207.1 5.5 %copy-start.4 = (f32[16,4,128]{2,1,0:T(4,128)S(1)}, f32[16,4,128]{2,1,0:T(4,128)}, u32[]{:S(2)}) copy-start(f32[16,4,128]{2,1,0:T(4,128)} %get-tuple-element.114) | copy-start | bytes 98308
  239.1 8.1 %copy-start.5 = (f32[16,4]{1,0:T(8,128)S(1)}, f32[16,4]{1,0:T(8,128)}, u32[]{:S(2)}) copy-start(f32[16,4]{1,0:T(8,128)} %copy.73) | copy-start | bytes 772
  239.2 8.1 %copy-start.6 = (f32[16,4]{1,0:T(8,128)S(1)}, f32[16,4]{1,0:T(8,128)}, u32[]{:S(2)}) copy-start(f32[16,4]{1,0:T(8,128)} %copy.72) | copy-start | bytes 772
  259.4 51.8 %slice-start = ((s8[6291456]{0:T(1024)(128)(4,1)}), s8[2097152]{0:T(1024)(128)(4,1)S(1)}, s32[]{:S(2)}) async-start(s8[6291456]{0:T(1024)(128)(4,1)} %bitcast.316), calls=%async_computation.4 | async-start | bytes 4194304
  262.3 48.9 %slice-start.1 = ((s8[6291456]{0:T(1024)(128)(4,1)}), s8[4194304]{0:T(1024)(128)(4,1)S(1)}, s32[]{:S(2)}) async-start(s8[6291456]{0:T(1024)(128)(4,1)} %bitcast.316), calls=%async_computation.5 | async-start | bytes 8388608
  282.5 28.7 %copy-start.7 = (f32[4096]{0:T(1024)S(1)}, f32[4096]{0:T(1024)}, u32[]{:S(2)}) copy-start(f32[4096]{0:T(1024)} %param.9) | copy-start | bytes 49156
where the time goes:
time: 318 us; the launch traced here: 314 us
  matrix products  161 us (51%)
  blocking collectives  48 us (15%)
  other arithmetic  37 us (12%)
  waiting for transfers between devices  35.3 us (11%)
  local copies, waits for them, and re-layouts  18.5 us (6%)
  starting transfers between devices  13 us (4%)
    dot_general x1, matrix products, middle_segment(): jnp.einsum('ckjs,sq->ckjq', mid_re, local_im, precision=HIGH)  44.3 us
    all_to_all x1, blocking collectives, on_device(): lax.all_to_all(lax.all_to_all(arranged.astype(jnp.bfloat16), 'outer', spl...  27.8 us
    all_to_all x1, waiting for transfers between devices, on_device(): lax.all_to_all(lax.all_to_all(sections.astype(jnp.bfloat16), 'outer', spl...  21.3 us
    all_to_all x1, blocking collectives, on_device(): lax.all_to_all(arranged.astype(jnp.bfloat16), 'outer', split_axis=3, conc...  20.2 us
    all_to_all x1, waiting for transfers between devices, on_device(): lax.all_to_all(sections.astype(jnp.bfloat16), 'outer', split_axis=0, conc...  14 us
    sub x2, other arithmetic, complex_times(): left_re * right_re - left_im * right_im  11.6 us
    dot_general x1, matrix products, middle_segment(): jnp.einsum('ji,ckis->ckjs', inner_im, sec_re, precision=HIGH)  10.3 us
    dot_general x1, matrix products, middle_segment(): jnp.einsum('ji,ckjs->ckis', inner_im, back_im, precision=HIGH)  9.72 us
  transfers between devices with their start and end apart: 3, of which 2 were waited for; matrix products, arithmetic and copies ran while one was open for 3% of the time, Pallas kernels for 0%

commit v1 on v0

v1 whole, which is shorter than its diff:
```python
import functools

import jax
import jax.numpy as jnp
from jax import lax
from jax.experimental import pallas as pl
from jax.experimental.pallas import tpu as pltpu
from jax.sharding import PartitionSpec as P

LANES = 128
SUB = 8
AXES = ("outer", "inner")
F32 = jnp.float32
BF16 = jnp.bfloat16


def column(group):
    return pl.ds(pl.multiple_of(group * LANES, LANES), LANES)


def featurize(pad_ref, block_ref, halo_ref, taps_ref, group):
    rows = block_ref.shape[0]
    cols = column(group)
    halo = halo_ref[:, cols].astype(F32)
    pad_ref[SUB - 2 : SUB, :] = halo
    pad_ref[SUB : SUB + rows, :] = block_ref[:, cols].astype(F32)
    taps = taps_ref[:, cols]
    return (
        taps[0:1] * pad_ref[SUB : SUB + rows, :]
        + taps[1:2] * pad_ref[SUB - 1 : SUB - 1 + rows, :]
        + taps[2:3] * pad_ref[SUB - 2 : SUB - 2 + rows, :]
    )


def state_kernel(k_ref, v_ref, hk_ref, hv_ref, tk_ref, tv_ref, rates_ref, mixed_ref, state_ref, pad_k, pad_v):
    rows, width = k_ref.shape
    modes = rates_ref.shape[0]
    place = lax.broadcasted_iota(jnp.int32, (SUB, LANES), 0).astype(F32)

    @pl.loop(0, width // LANES)
    def _(group):
        mixed = featurize(pad_k, k_ref, hk_ref, tk_ref, group) * featurize(
            pad_v, v_ref, hv_ref, tv_ref, group
        )
        mixed_ref[group] = mixed
        rates = rates_ref[:, column(group)]
        for mode in range(modes):
            rate = jnp.broadcast_to(rates[mode : mode + 1], (SUB, LANES))
            stride_decay = jnp.exp(-SUB * rate)
            total = mixed[0:SUB]
            for tile in range(1, rows // SUB):
                total = total * stride_decay + mixed[tile * SUB : (tile + 1) * SUB]
            total = total * jnp.exp(-rate * (SUB - 1 - place))
            state_ref[group, mode : mode + 1, :] = jnp.sum(total, 0, keepdims=True)


def scan_kernel(rows, got_ref, rates_ref, out_ref):
    decay = jnp.exp(-rows * rates_ref[...])

    def step(place, carry):
        out_ref[place] = carry.astype(BF16)
        return carry * decay + got_ref[place].astype(F32)

    lax.fori_loop(0, got_ref.shape[0], step, jnp.zeros(decay.shape, F32), unroll=4)


def local_kernel(mixed_ref, rates_ref, residues_ref, skip_ref, out_ref):
    groups, modes = SUB, rates_ref.shape[0]
    rows = mixed_ref.shape[0] // groups
    rates = [rates_ref[m] for m in range(modes)]
    decays = [jnp.exp(-r) for r in rates]
    gains = [residues_ref[m] * jnp.sqrt(2.0 * rates[m]) for m in range(modes)]
    skip = skip_ref[...]

    def step(token, states):
        at = pl.ds(token, groups, stride=rows)
        x = mixed_ref[at, :]
        states = tuple(s * d + x for s, d in zip(states, decays))
        terms = [s * g for s, g in zip(states, gains)] + [skip * x]
        while len(terms) > 1:
            terms = [a + b for a, b in zip(terms[::2], terms[1::2])] + (
                [terms[-1]] if len(terms) % 2 else []
            )
        out_ref[at, :] = terms[0]
        return states

    lax.fori_loop(0, rows, step, tuple(jnp.zeros((groups, LANES), F32) for _ in range(modes)), unroll=4)


def final_kernel(q_ref, hq_ref, tq_ref, local_ref, carry_ref, rates_ref, residues_ref, out_ref, pad_q):
    rows, width = q_ref.shape
    modes = rates_ref.shape[0]
    place = lax.broadcasted_iota(jnp.int32, (SUB, LANES), 0).astype(F32)

    @pl.loop(0, width // LANES)
    def _(group):
        cols = column(group)
        query = featurize(pad_q, q_ref, hq_ref, tq_ref, group)
        rates = rates_ref[:, cols]
        gains = residues_ref[:, cols] * jnp.sqrt(2.0 * rates) * carry_ref[group].astype(F32)
        strides, terms = [], []
        for mode in range(modes):
            rate = jnp.broadcast_to(rates[mode : mode + 1], (SUB, LANES))
            strides.append(jnp.exp(-SUB * rate))
            terms.append(jnp.exp(-rate * (place + 1.0)) * gains[mode : mode + 1])
        for tile in range(rows // SUB):
            at = slice(tile * SUB, (tile + 1) * SUB)
            level = terms
            while len(level) > 1:
                level = [a + b for a, b in zip(level[::2], level[1::2])] + (
                    [level[-1]] if len(level) % 2 else []
                )
            conv = level[0] + local_ref[group, at, :]
            pad_q[at, :] = query[at] * conv
            terms = [t * s for t, s in zip(terms, strides)]
        out_ref[:, cols] = pad_q[0:rows, :].astype(BF16)


def on_device(projected, short_taps, rates, residues, skip_gain):
    rows, feature_width = projected.shape
    channels = feature_width // 3
    modes = rates.shape[1]
    groups = channels // LANES
    count = lax.axis_size(AXES)
    place = lax.axis_index(AXES)
    own = channels // count
    halo = lax.ppermute(projected[rows - 2 :], AXES, [(s, s + 1) for s in range(count - 1)])
    rates_t, residues_t = rates.T, residues.T

    width = 4 * LANES
    steps = channels // width

    def part(which, height):
        return pl.BlockSpec((height, width), lambda i: (0, which * steps + i))

    by_group = lambda *inner: pl.BlockSpec((width // LANES, *inner), lambda i: (i, 0, 0))
    mixed, state = pl.pallas_call(
        state_kernel,
        grid=(steps,),
        in_specs=[part(1, rows), part(2, rows), part(1, 2), part(2, 2), part(1, 3), part(2, 3), part(0, modes)],
        out_specs=[by_group(rows, LANES), by_group(modes, LANES)],
        out_shape=[
            jax.ShapeDtypeStruct((groups, rows, LANES), F32),
            jax.ShapeDtypeStruct((groups, modes, LANES), F32),
        ],
        scratch_shapes=[pltpu.VMEM((rows + SUB, LANES), F32)] * 2,
        name="state",
    )(projected, projected, halo, halo, short_taps, short_taps, rates_t)

    def to_channels(x):
        x = x.astype(BF16)
        if own != LANES:
            x = jnp.moveaxis(x, 1, 0).reshape(modes, count, own)
            x = jnp.moveaxis(x, 1, 0)
        return x

    def to_groups(x):
        if own != LANES:
            x = jnp.moveaxis(x, 0, 1).reshape(modes, groups, LANES)
            x = jnp.moveaxis(x, 1, 0)
        return x

    got = lax.all_to_all(to_channels(state), AXES, split_axis=0, concat_axis=0, tiled=True)
    own_rates = lax.dynamic_slice_in_dim(rates_t, place * own, own, 1)
    scanned = pl.pallas_call(
        functools.partial(scan_kernel, rows),
        out_shape=jax.ShapeDtypeStruct((count, modes, own), BF16),
        name="scan",
    )(got, own_rates)
    carry = to_groups(lax.all_to_all(scanned, AXES, split_axis=0, concat_axis=0, tiled=True))

    wide = SUB * LANES
    local = pl.pallas_call(
        local_kernel,
        grid=(channels // wide,),
        in_specs=[
            pl.BlockSpec((SUB * rows, LANES), lambda i: (i, 0)),
            pl.BlockSpec((modes, SUB, LANES), lambda i: (0, i, 0)),
            pl.BlockSpec((modes, SUB, LANES), lambda i: (0, i, 0)),
            pl.BlockSpec((SUB, LANES), lambda i: (i, 0)),
        ],
        out_specs=pl.BlockSpec((SUB * rows, LANES), lambda i: (i, 0)),
        out_shape=jax.ShapeDtypeStruct((groups * rows, LANES), F32),
        cost_estimate=pl.CostEstimate(
            flops=4 * modes * rows * channels, bytes_accessed=8 * rows * channels, transcendentals=0
        ),
        name="local",
    )(
        mixed.reshape(groups * rows, LANES),
        rates_t.reshape(modes, groups, LANES),
        residues_t.reshape(modes, groups, LANES),
        skip_gain.reshape(groups, LANES),
    ).reshape(groups, rows, LANES)

    return pl.pallas_call(
        final_kernel,
        grid=(steps,),
        in_specs=[part(0, rows), part(0, 2), part(0, 3), by_group(rows, LANES), by_group(modes, LANES),
                  part(0, modes), part(0, modes)],
        out_specs=pl.BlockSpec((rows, width), lambda i: (0, i)),
        out_shape=jax.ShapeDtypeStruct((rows, channels), BF16),
        scratch_shapes=[pltpu.VMEM((rows + SUB, LANES), F32)],
        name="final",
    )(projected, halo, short_taps, local, carry, rates_t, residues_t)


def solution(mesh):
    in_specs = (P(AXES, None), P(), P(), P(), P())
    out_specs = P(AXES, None)
    return jax.shard_map(
        on_device, mesh=mesh, in_specs=in_specs, out_specs=out_specs, check_vma=False
    )
```

time: 318 us -> 57.4 us (0.18); the launches traced: 314 us -> 56.8 us
  matrix products: 161 us -> 0 us
  blocking collectives: 48 us -> 0 us
  other arithmetic: 37 us -> 1.62 us
  Pallas kernels: 0 us -> 26.5 us
  waiting for transfers between devices: 35.3 us -> 9.53 us
  local copies, waits for them, and re-layouts: 18.5 us -> 4.99 us
    dot_general x20 -> x0, matrix products: 161 us -> none  [the longest x1 44.3 us: middle_segment(): jnp.einsum('ckjs,sq->ckjq', mid_re, local_im, precision=HIGH)]
    all_to_all x2 -> x0, blocking collectives: 48 us -> none  [the longest x1 27.8 us: on_device(): lax.all_to_all(lax.all_to_all(arranged.astype(jnp.bfloat16), 'outer', spl...]
    all_to_all x2, waiting for transfers between devices: 35.3 us -> 7.8 us  [the longest x1 7.79 us: on_device(): lax.all_to_all(to_channels(state), AXES, split_axis=0, concat_axis=0, til...]
    pallas_call x0 -> x4, Pallas kernels: none -> 26.5 us  [the longest x1 9.22 us: on_device(): pl.pallas_call(local_kernel, grid=(channels // wide,), in_specs=[pl.Block...]
    add x3 -> x0, other arithmetic: 16.1 us -> none  [the longest x1 9.54 us: on_device(): short_taps[0] * padded[2:] + short_taps[1] * padded[1:-1]]
    sub x2 -> x0, other arithmetic: 11.6 us -> none  [complex_times(): left_re * right_re - left_im * right_im]
    convert_element_type x4 -> x1, other arithmetic: 5.39 us -> 1.62 us  [to_channels(): x = x.astype(BF16)]
    convert_element_type x3 -> x0, local copies, waits for them, and re-layouts: 3.5 us -> none  [the longest x1 1.79 us: on_device(): sections.astype(jnp.bfloat16)]
  transfers between devices with their start and end apart: 3 -> 3, of which waited for: 2 -> 2; matrix products, arithmetic and copies ran while one was open for 3% -> 4% of each run, Pallas kernels for 0% -> 16%
where the time goes in v1:
time: 57.4 us; the launch traced here: 56.8 us
  Pallas kernels  26.5 us (46%)
  starting transfers between devices  14.1 us (25%)
  waiting for transfers between devices  9.53 us (17%)
  local copies, waits for them, and re-layouts  4.99 us (9%)
  other arithmetic  1.62 us (3%)
    pallas_call x1, Pallas kernels, on_device(): pl.pallas_call(local_kernel, grid=(channels // wide,), in_specs=[pl.Block...  9.22 us
    pallas_call x1, Pallas kernels, on_device(): pl.pallas_call(state_kernel, grid=(steps,), in_specs=[part(1, rows), part...  8.15 us
    all_to_all x1, waiting for transfers between devices, on_device(): lax.all_to_all(to_channels(state), AXES, split_axis=0, concat_axis=0, til...  7.79 us
    pallas_call x1, Pallas kernels, on_device(): pl.pallas_call(final_kernel, grid=(steps,), in_specs=[part(0, rows), part...  7.47 us
    all_to_all x1, starting transfers between devices, on_device(): lax.all_to_all(to_channels(state), AXES, split_axis=0, concat_axis=0, til...  6.61 us
    ppermute x1, starting transfers between devices, on_device(): lax.ppermute(projected[rows - 2:], AXES, [(s, s + 1) for s in range(count...  4.93 us
    unnamed x12, local copies, waits for them, and re-layouts  3.42 us
    all_to_all x1, starting transfers between devices, on_device(): lax.all_to_all(scanned, AXES, split_axis=0, concat_axis=0, tiled=True)  2.56 us
  transfers between devices with their start and end apart: 3, of which 2 were waited for; matrix products, arithmetic and copies ran while one was open for 4% of the time, Pallas kernels for 16%

profile of v1, /device:TPU:0, one launch (start us, length us, event | category | flops | bytes accessed | tf_op | source)
XLA Modules:
  0.0 56.8 jit_solution(3300158138682133198)
XLA Ops:
  0.0 1.0 %slice.3 = bf16[2,12288]{1,0:T(2,128)(2,1)S(1)} slice(bf16[128,12288]{1,0:T(8,128)(2,1)} %q_ref.1), slice={[126:128], [0:12288]} | slice | bytes 98304 | tf_op jit(solution)/shard_map/slice | solution.py:127
  1.0 4.9 %collective-permute-start = (bf16[2,12288]{1,0:T(2,128)(2,1)S(1)}, bf16[2,12288]{1,0:T(2,128)(2,1)S(1)}, u32[]{:S(2)}, u32[]{:S(2)}) collective-permute-start(bf16[2,12288]{1,0:T(2,128)(2,1)S(1)} %slice.3), channel_id=1, source_target_pairs={{0,1},{1,2},{2,3},{3,4},{4,5},{5,6},{6,7},{7,8},{8,9},{9,10},{10,1... | collective-permute-start | bytes 147464 | tf_op jit(solution)/shard_map/ppermute | solution.py:127
  5.9 1.7 %collective-permute-done.hk_ref.hv_ref.hq_ref = bf16[2,12288]{1,0:T(2,128)(2,1)S(1)} collective-permute-done((bf16[2,12288]{1,0:T(2,128)(2,1)S(1)}, bf16[2,12288]{1,0:T(2,128)(2,1)S(1)}, u32[]{:S(2)}, u32[]{:S(2)}) %collective-permute-start) | collective-permute-done | bytes 49184 | tf_op jit(solution)/shard_map/ppermute | solution.py:127
  7.7 0.0 copy-start.4
  7.7 0.6 %copy-done.4 = bf16[2,12288]{1,0:T(2,128)(2,1)} copy-done((bf16[2,12288]{1,0:T(2,128)(2,1)}, bf16[2,12288]{1,0:T(2,128)(2,1)S(1)}, u32[]{:S(2)}) %copy-start.4) | copy-done | bytes 49176
  8.3 0.0 copy-start
  8.3 0.0 copy-start.1
  8.3 8.2 %state.1 = (f32[32,128,128]{2,1,0:T(8,128)}, f32[32,16,128]{2,1,0:T(8,128)}) custom-call(bf16[128,12288]{1,0:T(8,128)(2,1)} %q_ref.1, bf16[128,12288]{1,0:T(8,128)(2,1)} %q_ref.1, bf16[2,12288]{1,0:T(2,128)(2,1)} %copy-done.4, bf16[2,12288]{1,0:T(2,128)(2,1)} %copy-done.4, f32[3,12288]{1,0:T(4,128)} %tq_ref.1, f32[3,12288]{1,0:T(4,128)} %tq_ref.1, ...), custom_call_target="tpu_custom_call" | custom-call | tf_op jit(solution)/shard_map/state/pallas_call | solution.py:137
  16.4 1.6 %convert_element_type.3 = bf16[32,16,128]{2,1,0:T(8,128)(2,1)} convert(f32[32,16,128]{2,1,0:T(8,128)} %get-tuple-element.8) | non-fusion elementwise | flops 65536 | bytes 393216 | tf_op jit(solution)/shard_map/convert_element_type | solution.py:151
  18.0 6.6 %all-to-all-start = ((bf16[32,16,128]{2,1,0:T(8,128)(2,1)}), bf16[32,16,128]{2,1,0:T(8,128)(2,1)S(1)}, u32[]{:S(2)}, u32[]{:S(2)}) async-start(bf16[32,16,128]{2,1,0:T(8,128)(2,1)} %convert_element_type.3), calls=%async_computation | async-start | bytes 262144 | tf_op jit(solution)/shard_map/all_to_all | solution.py:163
  24.7 0.0 copy-done
  24.7 0.6 %dynamic-slice_bitcast_fusion.rates_ref = f32[16,128]{1,0:T(8,128)} fusion(f32[4096,16]{0,1:T(8,128)S(1)} %copy-done, s32[]{:T(128)S(6)} %select_n.3), kind=kLoop, calls=%fused_computation | loop fusion | bytes 16388 | tf_op jit(solution)/shard_map/dynamic_slice | solution.py:164
  25.3 7.8 %all-to-all-done.got_ref = bf16[32,16,128]{2,1,0:T(8,128)(2,1)S(1)} async-done(((bf16[32,16,128]{2,1,0:T(8,128)(2,1)}), bf16[32,16,128]{2,1,0:T(8,128)(2,1)S(1)}, u32[]{:S(2)}, u32[]{:S(2)}) %all-to-all-start) | async-done | bytes 131104 | tf_op jit(solution)/shard_map/all_to_all | solution.py:163
  33.1 0.0 copy-start.3
  33.1 0.7 %copy-done.3 = bf16[32,16,128]{2,1,0:T(8,128)(2,1)} copy-done((bf16[32,16,128]{2,1,0:T(8,128)(2,1)}, bf16[32,16,128]{2,1,0:T(8,128)(2,1)S(1)}, u32[]{:S(2)}) %copy-start.3) | copy-done | bytes 131096
  33.7 1.7 %scan.1 = bf16[32,16,128]{2,1,0:T(8,128)(2,1)} custom-call(bf16[32,16,128]{2,1,0:T(8,128)(2,1)} %copy-done.3, f32[16,128]{1,0:T(8,128)} %dynamic-slice_bitcast_fusion.rates_ref), custom_call_target="tpu_custom_call" | custom-call | tf_op jit(solution)/shard_map/scan/pallas_call | solution.py:165
  35.4 2.6 %all-to-all-start.1 = ((bf16[32,16,128]{2,1,0:T(8,128)(2,1)}), bf16[32,16,128]{2,1,0:T(8,128)(2,1)S(1)}, u32[]{:S(2)}, u32[]{:S(2)}) async-start(bf16[32,16,128]{2,1,0:T(8,128)(2,1)} %scan.1), calls=%async_computation.1 | async-start | bytes 262144 | tf_op jit(solution)/shard_map/all_to_all | solution.py:170
  37.9 0.8 %copy.6 = f32[2,8,32,128]{3,2,1,0:T(8,128)} copy(f32[2,8,32,128]{3,1,2,0:T(8,128)S(1)} %bitcast.14) | data formatting | bytes 524288
  38.7 0.0 copy-done.1
  38.7 0.7 %copy.7 = f32[2,8,32,128]{3,2,1,0:T(8,128)} copy(f32[2,8,32,128]{3,1,2,0:T(8,128)S(1)} %bitcast.17) | data formatting | bytes 524288
  39.4 9.2 %local.1 = f32[4096,128]{1,0:T(8,128)} custom-call(f32[4096,128]{1,0:T(8,128)} %bitcast.15, f32[16,32,128]{2,1,0:T(8,128)} %bitcast.18, f32[16,32,128]{2,1,0:T(8,128)} %bitcast.19, f32[32,128]{1,0:T(8,128)} %bitcast.20), custom_call_target="tpu_custom_call" | custom-call | flops 33554432 | bytes 4194304 | tf_op jit(solution)/shard_map/local/pallas_call | solution.py:173
  48.7 0.0 all-to-all-done.1.carry_ref
  48.7 0.0 copy-start.2
  48.7 0.6 %copy-done.2 = bf16[32,16,128]{2,1,0:T(8,128)(2,1)} copy-done((bf16[32,16,128]{2,1,0:T(8,128)(2,1)}, bf16[32,16,128]{2,1,0:T(8,128)(2,1)S(1)}, u32[]{:S(2)}) %copy-start.2) | copy-done | bytes 131096
  49.3 7.5 %final.1 = bf16[128,4096]{1,0:T(8,128)(2,1)} custom-call(bf16[128,12288]{1,0:T(8,128)(2,1)} %q_ref.1, bf16[2,12288]{1,0:T(2,128)(2,1)} %copy-done.4, f32[3,12288]{1,0:T(4,128)} %tq_ref.1, f32[32,128,128]{2,1,0:T(8,128)} %bitcast.11, bf16[32,16,128]{2,1,0:T(8,128)(2,1)} %copy-done.2, f32[16,4096]{1,0:T(8,128)} %bitcast.13, f32[16,4096]{1,0:T(8,128)} %bitcast.16), custom_call_target="tpu_custom_call" | custom-call | tf_op jit(solution)/shard_map/final/pallas_call | solution.py:195
Async XLA Ops:
  1.0 6.7 %collective-permute-start = (bf16[2,12288]{1,0:T(2,128)(2,1)S(1)}, bf16[2,12288]{1,0:T(2,128)(2,1)S(1)}, u32[]{:S(2)}, u32[]{:S(2)}) collective-permute-start(bf16[2,12288]{1,0:T(2,128)(2,1)S(1)} %slice.3), channel_id=1, source_target_pairs={{0,1},{1,2},{2,3},{3,4},{4,5},{5,6},{6,7},{7,8},{8,9},{9,10},{10,1... | collective-permute-start | bytes 147464 | tf_op jit(solution)/shard_map/ppermute | solution.py:127
  7.7 0.6 %copy-start.4 = (bf16[2,12288]{1,0:T(2,128)(2,1)}, bf16[2,12288]{1,0:T(2,128)(2,1)S(1)}, u32[]{:S(2)}) copy-start(bf16[2,12288]{1,0:T(2,128)(2,1)S(1)} %collective-permute-done.hk_ref.hv_ref.hq_ref) | copy-start | bytes 147460
  8.3 16.4 %copy-start = (f32[4096,16]{0,1:T(8,128)S(1)}, f32[4096,16]{0,1:T(8,128)}, u32[]{:S(2)}) copy-start(f32[4096,16]{0,1:T(8,128)} %param.7) | copy-start | bytes 786436
  8.3 30.4 %copy-start.1 = (f32[4096,16]{0,1:T(8,128)S(1)}, f32[4096,16]{0,1:T(8,128)}, u32[]{:S(2)}) copy-start(f32[4096,16]{0,1:T(8,128)} %param.8) | copy-start | bytes 786436
  18.0 15.0 %all-to-all-start = ((bf16[32,16,128]{2,1,0:T(8,128)(2,1)}), bf16[32,16,128]{2,1,0:T(8,128)(2,1)S(1)}, u32[]{:S(2)}, u32[]{:S(2)}) async-start(bf16[32,16,128]{2,1,0:T(8,128)(2,1)} %convert_element_type.3), calls=%async_computation | async-start | bytes 262144 | tf_op jit(solution)/shard_map/all_to_all | solution.py:163
  33.1 0.7 %copy-start.3 = (bf16[32,16,128]{2,1,0:T(8,128)(2,1)}, bf16[32,16,128]{2,1,0:T(8,128)(2,1)S(1)}, u32[]{:S(2)}) copy-start(bf16[32,16,128]{2,1,0:T(8,128)(2,1)S(1)} %all-to-all-done.got_ref) | copy-start | bytes 393220
  35.4 13.3 %all-to-all-start.1 = ((bf16[32,16,128]{2,1,0:T(8,128)(2,1)}), bf16[32,16,128]{2,1,0:T(8,128)(2,1)S(1)}, u32[]{:S(2)}, u32[]{:S(2)}) async-start(bf16[32,16,128]{2,1,0:T(8,128)(2,1)} %scan.1), calls=%async_computation.1 | async-start | bytes 262144 | tf_op jit(solution)/shard_map/all_to_all | solution.py:170
  48.7 0.6 %copy-start.2 = (bf16[32,16,128]{2,1,0:T(8,128)(2,1)}, bf16[32,16,128]{2,1,0:T(8,128)(2,1)S(1)}, u32[]{:S(2)}) copy-start(bf16[32,16,128]{2,1,0:T(8,128)(2,1)S(1)} %all-to-all-done.1.carry_ref) | copy-start | bytes 393220

commit v2 on v1

v2 whole, which is shorter than its diff:
```python
import functools

import jax
import jax.numpy as jnp
from jax import lax
from jax.experimental import pallas as pl
from jax.experimental.pallas import tpu as pltpu
from jax.sharding import PartitionSpec as P

LANES = 128
SUB = 8
PIECES = 4
AXES = ("outer", "inner")
F32 = jnp.float32
BF16 = jnp.bfloat16
HBM = pl.BlockSpec(memory_space=pl.ANY)
VMEM = pl.BlockSpec(memory_space=pltpu.VMEM)
PARAMS = pltpu.CompilerParams(vmem_limit_bytes=32 * 1024 * 1024)


def held(x):
    return pltpu.with_memory_space_constraint(x, pltpu.VMEM)


def column(group):
    return pl.ds(pl.multiple_of(group * LANES, LANES), LANES)


def tree_sum(terms):
    while len(terms) > 1:
        terms = [a + b for a, b in zip(terms[::2], terms[1::2])] + ([terms[-1]] if len(terms) % 2 else [])
    return terms[0]


def short_filter(pad_ref, taps, rows):
    return (
        taps[0:1] * pad_ref[SUB : SUB + rows, :]
        + taps[1:2] * pad_ref[SUB - 1 : SUB - 1 + rows, :]
        + taps[2:3] * pad_ref[SUB - 2 : SUB - 2 + rows, :]
    )


def sublane():
    return lax.broadcasted_iota(jnp.int32, (SUB, LANES), 0)


def state_kernel(proj_ref, taps_hbm, rates_hbm, sent_ref, mixed_ref, k_buf, v_buf, taps_ref, rates_ref, table, ends, pad_k, pad_v, sems, more):
    rows, channels = k_buf.shape
    modes = rates_ref.shape[0]
    groups = channels // LANES
    wide = channels // PIECES
    whole = [pltpu.make_async_copy(rates_hbm, rates_ref, more.at[0]), pltpu.make_async_copy(taps_hbm, taps_ref, more.at[1])]
    pieces = []
    for piece in range(PIECES):
        at = pl.ds(piece * wide, wide)
        pieces.append([
            pltpu.make_async_copy(proj_ref.at[:, pl.ds(channels + piece * wide, wide)], k_buf.at[:, at], sems.at[0, piece]),
            pltpu.make_async_copy(proj_ref.at[:, pl.ds(2 * channels + piece * wide, wide)], v_buf.at[:, at], sems.at[1, piece]),
        ])
    for copy in whole + [c for pair in pieces for c in pair]:
        copy.start()
    whole[0].wait()
    decay = jnp.exp(-rates_ref[...])
    for power in range(4):
        table[power] = decay
        decay = decay * decay
    whole[1].wait()
    row = sublane()
    for piece in range(PIECES):
        for copy in pieces[piece]:
            copy.wait()

        @pl.loop(piece * (groups // PIECES), (piece + 1) * (groups // PIECES))
        def _(group):
            cols = column(group)
            pad_k[SUB : SUB + rows, :] = k_buf[:, cols].astype(F32)
            pad_v[SUB : SUB + rows, :] = v_buf[:, cols].astype(F32)
            mixed = short_filter(pad_k, taps_ref[:, column(groups + group)], rows) * short_filter(
                pad_v, taps_ref[:, column(2 * groups + group)], rows
            )
            tiles = [mixed[i * SUB : (i + 1) * SUB] for i in range(rows // SUB)]
            tiles[0] = jnp.where(row < 2, 0.0, tiles[0])
            for i, tile in enumerate(tiles):
                mixed_ref[pl.ds(pl.multiple_of(group * rows + i * SUB, SUB), SUB), :] = tile
            for mode in range(modes):
                one, two, four, eight = (
                    jnp.broadcast_to(table[power, mode : mode + 1, cols], (SUB, LANES)) for power in range(4)
                )
                total = tiles[0]
                for tile in tiles[1:]:
                    total = total * eight + tile
                total = total + four * pltpu.roll(total, 4, 0)
                total = total + two * pltpu.roll(total, 2, 0)
                total = total + one * pltpu.roll(total, 1, 0)
                ends[mode : mode + 1, :] = total[SUB - 1 :]
            first_k, first_v = pad_k[SUB : 2 * SUB, :], pad_v[SUB : 2 * SUB, :]
            last_k, last_v = pad_k[rows : SUB + rows, :], pad_v[rows : SUB + rows, :]
            ends[modes:, :] = jnp.where(
                row < 2,
                first_k,
                jnp.where(row < 4, pltpu.roll(first_v, 2, 0), jnp.where(row < 6, pltpu.roll(last_k, 6, 0), last_v)),
            )
            sent_ref[group] = ends[...].astype(BF16)


def scan_kernel(rows, modes, got_ref, rates_ref, tk_ref, tv_ref, out_ref):
    one = jnp.exp(-rates_ref[...])
    two = jnp.exp(-2.0 * rates_ref[...])
    rest = jnp.exp(-(rows - 2.0) * rates_ref[...])
    row = sublane()
    taps = [jnp.where(row < 2, tk_ref[i : i + 1, :], tv_ref[i : i + 1, :]) for i in range(3)]

    def step(place, carry):
        state, before = carry
        edge = got_ref[place, modes:, :].astype(F32)
        feat = (
            taps[0] * edge
            + taps[1] * jnp.where(row % 2 == 1, pltpu.roll(edge, 1, 0), pltpu.roll(before, 3, 0))
            + taps[2] * pltpu.roll(before, 4, 0)
        )
        mixed = feat * pltpu.roll(feat, SUB - 2, 0)
        state = state * two + one * mixed[0:1] + mixed[1:2]
        out_ref[place] = state.astype(BF16)
        return state * rest + got_ref[place, :modes, :].astype(F32), edge

    first = (jnp.zeros((modes, LANES), F32), jnp.zeros((SUB, LANES), F32))
    lax.fori_loop(0, got_ref.shape[0], step, first, unroll=8)


def recur(rows, first, blocks, mixed_ref, rates_ref, residues_ref, skip_ref, out_ref):
    modes = rates_ref.shape[0]

    @pl.loop(0, blocks)
    def _(block):
        chosen = pl.ds(pl.multiple_of((first + block) * SUB, SUB), SUB)
        rates = [rates_ref[m, chosen, :] for m in range(modes)]
        decays = [jnp.exp(-r) for r in rates]
        gains = [residues_ref[m, chosen, :] * jnp.sqrt(2.0 * rates[m]) for m in range(modes)]
        skip = skip_ref[chosen, :]

        def step(token, states):
            x = mixed_ref[pl.ds((first + block) * SUB * rows + token, SUB, stride=rows), :]
            states = tuple(s * d + x for s, d in zip(states, decays))
            out_ref[pl.ds(block * SUB * rows + token, SUB, stride=rows), :] = tree_sum(
                [s * g for s, g in zip(states, gains)] + [skip * x]
            )
            return states

        lax.fori_loop(0, rows, step, tuple(jnp.zeros((SUB, LANES), F32) for _ in range(modes)), unroll=4)


def early_kernel(blocks, proj_ref, mixed_ref, rates_ref, residues_ref, skip_ref, out_ref, tail_ref, buf, sem):
    rows = proj_ref.shape[0]
    copy = pltpu.make_async_copy(proj_ref.at[pl.ds(rows - 2 * SUB, 2 * SUB), :], buf, sem)
    copy.start()
    recur(rows, 0, blocks, mixed_ref, rates_ref, residues_ref, skip_ref, out_ref)
    copy.wait()
    tail_ref[...] = buf[2 * SUB - 2 :, :]


def late_kernel(
    first, blocks, proj_ref, halo_ref, after_ref, mixed_ref, rates_ref, residues_ref, skip_ref, taps_ref, flat_rates_ref, flat_residues_ref,
    out_ref, query_ref, start_ref, stride_ref, edge_ref, q_buf, head_buf, pad, sems,
):
    rows, channels = q_buf.shape
    modes = rates_ref.shape[0]
    groups = channels // LANES
    copies = [
        pltpu.make_async_copy(proj_ref.at[:, pl.ds(0, channels)], q_buf, sems.at[0]),
        pltpu.make_async_copy(proj_ref.at[pl.ds(0, 2 * SUB), pl.ds(channels, 2 * channels)], head_buf, sems.at[1]),
    ]
    for copy in copies:
        copy.start()
    recur(rows, first, blocks, mixed_ref, rates_ref, residues_ref, skip_ref, out_ref)
    for copy in copies:
        copy.wait()
    row = sublane()
    place = row.astype(F32) - 1.0

    @pl.loop(0, groups)
    def _(group):
        cols = column(group)
        pad[SUB - 2 : SUB, :] = halo_ref[:, cols].astype(F32)
        pad[SUB : SUB + rows, :] = q_buf[:, cols].astype(F32)
        query_ref[pl.ds(pl.multiple_of(group * rows, rows), rows), :] = short_filter(pad, taps_ref[:, cols], rows)
        rates = flat_rates_ref[:, cols]
        gains = flat_residues_ref[:, cols] * jnp.sqrt(2.0 * rates)
        stride_ref[group] = jnp.exp(-SUB * rates)
        starts = [jnp.exp(-rates[m : m + 1] * place) * gains[m : m + 1] for m in range(modes)]
        for mode in range(modes):
            start_ref[group, mode] = starts[mode]
        mixed = None
        for which in (1, 2):
            at = column(which * groups + group)
            pad[SUB - 2 : SUB, :] = halo_ref[:, at].astype(F32)
            pad[SUB : 3 * SUB, :] = head_buf[:, column((which - 1) * groups + group)].astype(F32)
            feat = short_filter(pad, taps_ref[:, at], SUB)
            mixed = feat if mixed is None else mixed * feat
        skip = skip_ref[pl.ds(group, 1), :]
        own = skip * mixed - jnp.where(row == 0, tree_sum(starts) * pltpu.roll(mixed, SUB - 1, 0), 0.0)
        edge_ref[group] = jnp.where(row < 2, own, 0.0)


def final_kernel(carry_ref, early_ref, late_ref, query_ref, start_ref, stride_ref, edge_ref, out_hbm, out_buf, sems):
    rows, channels = out_buf.shape
    groups, modes = stride_ref.shape[0], stride_ref.shape[1]
    split = early_ref.shape[0] // rows
    copies = []
    for piece in range(PIECES):
        low, high = piece * groups // PIECES, (piece + 1) * groups // PIECES
        local_ref, base = (early_ref, 0) if high <= split else (late_ref, split)

        @pl.loop(low, high)
        def _(group):
            carry = carry_ref[group].astype(F32)
            strides = [jnp.broadcast_to(stride_ref[group, m : m + 1, :], (SUB, LANES)) for m in range(modes)]
            terms = [start_ref[group, m] * carry[m : m + 1] for m in range(modes)]
            made = []
            for tile in range(rows // SUB):
                own = local_ref[pl.ds(pl.multiple_of((group - base) * rows + tile * SUB, SUB), SUB), :]
                if tile == 0:
                    own = own + edge_ref[group]
                query = query_ref[pl.ds(pl.multiple_of(group * rows + tile * SUB, SUB), SUB), :]
                made.append(query * (tree_sum(terms) + own))
                if tile + 1 < rows // SUB:
                    terms = [t * s for t, s in zip(terms, strides)]
            for i in range(0, len(made), 2):
                out_buf[i * SUB : (i + 2) * SUB, column(group)] = jnp.concatenate(made[i : i + 2], 0).astype(BF16)

        at = pl.ds(low * LANES, (high - low) * LANES)
        copies.append(pltpu.make_async_copy(out_buf.at[:, at], out_hbm.at[:, at], sems.at[piece]))
        copies[-1].start()
    for copy in copies:
        copy.wait()


def on_device(projected, short_taps, rates, residues, skip_gain):
    rows, feature_width = projected.shape
    channels = feature_width // 3
    modes = rates.shape[1]
    groups = channels // LANES
    count = lax.axis_size(AXES)
    place = lax.axis_index(AXES)
    own = channels // count
    rates_t, residues_t = rates.T, residues.T
    sent_rows = modes + SUB
    edge_dma = pltpu.SemaphoreType.DMA

    sent, mixed = pl.pallas_call(
        state_kernel,
        in_specs=[HBM, HBM, HBM],
        out_specs=[VMEM, VMEM],
        out_shape=[pltpu.VMEM((groups, sent_rows, LANES), BF16), pltpu.VMEM((groups * rows, LANES), F32)],
        scratch_shapes=[
            pltpu.VMEM((rows, channels), BF16),
            pltpu.VMEM((rows, channels), BF16),
            pltpu.VMEM(short_taps.shape, F32),
            pltpu.VMEM((modes, channels), F32),
            pltpu.VMEM((4, modes, channels), F32),
            pltpu.VMEM((sent_rows, LANES), F32),
            pltpu.VMEM((rows + SUB, LANES), F32),
            pltpu.VMEM((rows + SUB, LANES), F32),
            edge_dma((2, PIECES)),
            edge_dma((2,)),
        ],
        compiler_params=PARAMS,
        name="state",
    )(projected, short_taps, rates_t)

    def exchange(x):
        return lax.all_to_all(x, AXES, split_axis=0, concat_axis=0, tiled=True)

    if own == LANES:
        got = exchange(sent)
    else:
        parts = sent.reshape(groups, sent_rows, LANES // own, own).transpose(0, 2, 1, 3)
        got = exchange(parts.reshape(count, sent_rows, own))
        got = jnp.pad(got, ((0, 0), (0, 0), (0, LANES - own)))

    def own_part(x, start=0):
        part = lax.dynamic_slice_in_dim(x, start + place * own, own, 1)
        return part if own == LANES else jnp.pad(part, ((0, 0), (0, LANES - own)))

    scanned = pl.pallas_call(
        functools.partial(scan_kernel, rows, modes),
        in_specs=[VMEM] * 4,
        out_specs=VMEM,
        out_shape=pltpu.VMEM((count, modes, LANES), BF16),
        compiler_params=PARAMS,
        name="scan",
    )(held(got), own_part(rates_t), own_part(short_taps, channels), own_part(short_taps, 2 * channels))
    if own == LANES:
        carry = exchange(scanned)
    else:
        parts = exchange(scanned[:, :, :own]).reshape(groups, LANES // own, modes, own)
        carry = parts.transpose(0, 2, 1, 3).reshape(groups, modes, LANES)

    by_group = lambda x: x.reshape(modes, groups, LANES)
    skip = skip_gain.reshape(groups, LANES)
    blocks = groups // SUB
    early_blocks = blocks // 2
    early, tail = pl.pallas_call(
        functools.partial(early_kernel, early_blocks),
        in_specs=[HBM, VMEM, VMEM, VMEM, VMEM],
        out_specs=[VMEM, VMEM],
        out_shape=[
            pltpu.VMEM((early_blocks * SUB * rows, LANES), F32),
            pltpu.VMEM((2, feature_width), BF16),
        ],
        scratch_shapes=[pltpu.VMEM((2 * SUB, feature_width), BF16), edge_dma],
        cost_estimate=pl.CostEstimate(flops=2 * modes * rows * channels, bytes_accessed=4 * rows * channels, transcendentals=0),
        compiler_params=PARAMS,
        name="early",
    )(projected, held(mixed), by_group(rates_t), by_group(residues_t), skip)
    halo = lax.ppermute(tail, AXES, [(s, s + 1) for s in range(count - 1)])

    late_blocks = blocks - early_blocks
    late, query, start, stride, edge = pl.pallas_call(
        functools.partial(late_kernel, early_blocks, late_blocks),
        in_specs=[HBM, VMEM, HBM] + [VMEM] * 7,
        out_specs=[VMEM] * 5,
        out_shape=[
            pltpu.VMEM((late_blocks * SUB * rows, LANES), F32),
            pltpu.VMEM((groups * rows, LANES), F32),
            pltpu.VMEM((groups, modes, SUB, LANES), F32),
            pltpu.VMEM((groups, modes, LANES), F32),
            pltpu.VMEM((groups, SUB, LANES), F32),
        ],
        scratch_shapes=[
            pltpu.VMEM((rows, channels), BF16),
            pltpu.VMEM((2 * SUB, 2 * channels), BF16),
            pltpu.VMEM((rows + SUB, LANES), F32),
            edge_dma((2,)),
        ],
        cost_estimate=pl.CostEstimate(flops=2 * modes * rows * channels, bytes_accessed=4 * rows * channels, transcendentals=0),
        compiler_params=PARAMS,
        name="late",
    )(projected, held(halo), scanned, held(mixed), by_group(rates_t), by_group(residues_t), skip, short_taps, rates_t, residues_t)

    return pl.pallas_call(
        final_kernel,
        in_specs=[VMEM] * 7,
        out_specs=HBM,
        out_shape=jax.ShapeDtypeStruct((rows, channels), BF16),
        scratch_shapes=[pltpu.VMEM((rows, channels), BF16), edge_dma((PIECES,))],
        compiler_params=PARAMS,
        name="final",
    )(held(carry), held(early), held(late), held(query), held(start), held(stride), held(edge))


def solution(mesh):
    in_specs = (P(AXES, None), P(), P(), P(), P())
    out_specs = P(AXES, None)
    return jax.shard_map(
        on_device, mesh=mesh, in_specs=in_specs, out_specs=out_specs, check_vma=False
    )
```

time: 57.4 us -> 69.3 us (1.21)
  the two profiles are of different devices: /device:TPU:0 before, /device:TPU:4 now
where the time goes in v2:
time: 69.3 us; the launch traced here: 68.7 us
  local copies, waits for them, and re-layouts  22.6 us (33%)
  Pallas kernels  19.7 us (28%)
  waiting for transfers between devices  13.4 us (19%)
  starting transfers between devices  12.9 us (19%)
    unnamed x48, local copies, waits for them, and re-layouts  21.9 us
    all_to_all x2, starting transfers between devices, exchange(): return lax.all_to_all(x, AXES, split_axis=0, concat_axis=0, tiled=True)  9.45 us
    all_to_all x2, waiting for transfers between devices, exchange(): return lax.all_to_all(x, AXES, split_axis=0, concat_axis=0, tiled=True)  7.81 us
    pallas_call x1, Pallas kernels, on_device(): pl.pallas_call(functools.partial(late_kernel, early_blocks, late_blocks),...  5.62 us
    ppermute x1, waiting for transfers between devices, on_device(): halo = lax.ppermute(tail, AXES, [(s, s + 1) for s in range(count - 1)])  5.56 us
    pallas_call x1, Pallas kernels, on_device(): pl.pallas_call(state_kernel, in_specs=[HBM, HBM, HBM], out_specs=[VMEM, V...  5.06 us
    pallas_call x1, Pallas kernels, on_device(): pl.pallas_call(functools.partial(early_kernel, early_blocks), in_specs=[H...  3.84 us
    ppermute x1, starting transfers between devices, on_device(): halo = lax.ppermute(tail, AXES, [(s, s + 1) for s in range(count - 1)])  3.43 us
  transfers between devices with their start and end apart: 3, of which 2 were waited for; matrix products, arithmetic and copies ran while one was open for 3% of the time, Pallas kernels for 14%

profile of v2, /device:TPU:4, one launch (start us, length us, event | category | flops | bytes accessed | tf_op | source)
XLA Modules:
  0.0 68.7 jit_solution(3307449786092162651)
XLA Ops:
  0.0 0.0 copy-start
  0.0 1.9 %copy-done = bf16[128,12288]{1,0:T(8,128)(2,1)S(1)} copy-done((bf16[128,12288]{1,0:T(8,128)(2,1)S(1)}, bf16[128,12288]{1,0:T(8,128)(2,1)}, u32[]{:S(2)}) %copy-start) | copy-done | bytes 3145752
  1.9 0.0 copy-start.4
  1.9 0.9 %copy-done.4 = f32[4096,16]{0,1:T(8,128)S(1)} copy-done((f32[4096,16]{0,1:T(8,128)S(1)}, f32[4096,16]{0,1:T(8,128)}, u32[]{:S(2)}) %copy-start.4) | copy-done | bytes 262168
  2.8 0.0 copy-start.15
  2.8 0.9 %copy-done.15 = f32[3,12288]{1,0:T(4,128)S(1)} copy-done((f32[3,12288]{1,0:T(4,128)S(1)}, f32[3,12288]{1,0:T(4,128)}, u32[]{:S(2)}) %copy-start.15) | copy-done | bytes 147480
  3.8 0.0 copy-start.5
  3.8 0.0 copy-start.1
  3.8 0.0 copy-start.22
  3.8 5.1 %state.1 = (bf16[32,24,128]{2,1,0:T(8,128)(2,1)S(1)}, f32[4096,128]{1,0:T(8,128)S(1)}) custom-call(bf16[128,12288]{1,0:T(8,128)(2,1)S(1)} %copy-done, f32[3,12288]{1,0:T(4,128)S(1)} %copy-done.15, f32[16,4096]{1,0:T(8,128)S(1)} %bitcast.9), custom_call_target="tpu_custom_call" | custom-call | tf_op jit(solution)/shard_map/state/pallas_call | solution.py:249
  8.8 0.0 copy-start.2
  8.9 1.3 %copy-done.2 = f32[4096,128]{1,0:T(8,128)} copy-done((f32[4096,128]{1,0:T(8,128)}, f32[4096,128]{1,0:T(8,128)S(1)}, u32[]{:S(2)}) %copy-start.2) | copy-done | bytes 2097176
  10.2 0.0 copy-start.19
  10.2 0.7 copy-done.19
  10.9 6.1 %all-to-all-start = ((bf16[32,24,128]{2,1,0:T(8,128)(2,1)}), bf16[32,24,128]{2,1,0:T(8,128)(2,1)}, u32[]{:S(2)}, u32[]{:S(2)}) async-start(bf16[32,24,128]{2,1,0:T(8,128)(2,1)} %copy-done.19), calls=%async_computation | async-start | bytes 393216 | tf_op jit(solution)/shard_map/all_to_all | solution.py:271
  17.0 0.7 %constant_dynamic-slice_fusion = (f32[3,128]{1,0:T(4,128)S(1)}, f32[3,128]{1,0:T(4,128)S(1)}) fusion(f32[3,12288]{1,0:T(4,128)} %taps_ref.1, s32[]{:T(128)S(6)} %select_n.11, s32[]{:T(128)S(6)} %select_n.10), kind=kLoop, calls=%fused_computation.1 | loop fusion | bytes 6152 | tf_op jit(solution)/shard_map/dynamic_slice | solution.py:281
  17.7 0.0 copy-done.5
  17.7 7.8 %all-to-all-done.got_ref = bf16[32,24,128]{2,1,0:T(8,128)(2,1)} async-done(((bf16[32,24,128]{2,1,0:T(8,128)(2,1)}), bf16[32,24,128]{2,1,0:T(8,128)(2,1)}, u32[]{:S(2)}, u32[]{:S(2)}) %all-to-all-start) | async-done | bytes 196640 | tf_op jit(solution)/shard_map/all_to_all | solution.py:271
  25.6 1.8 %scan.1.after_ref = bf16[32,16,128]{2,1,0:T(8,128)(2,1)} custom-call(bf16[32,24,128]{2,1,0:T(8,128)(2,1)} %all-to-all-done.got_ref, f32[16,128]{1,0:T(8,128)S(1)} %dynamic-slice_bitcast_fusion.rates_ref, f32[3,128]{1,0:T(4,128)S(1)} %get-tuple-element.24.tk_ref, f32[3,128]{1,0:T(4,128)S(1)} %get-tuple-element.23.tv_ref), custom_call_target="tpu_custom_call" | custom-call | tf_op jit(solution)/shard_map/scan/pallas_call | solution.py:284
  27.4 3.3 %all-to-all-start.1 = ((bf16[32,16,128]{2,1,0:T(8,128)(2,1)}), bf16[32,16,128]{2,1,0:T(8,128)(2,1)S(1)}, u32[]{:S(2)}, u32[]{:S(2)}) async-start(bf16[32,16,128]{2,1,0:T(8,128)(2,1)} %scan.1.after_ref), calls=%async_computation.1 | async-start | bytes 262144 | tf_op jit(solution)/shard_map/all_to_all | solution.py:271
  30.7 0.1 copy.6
  30.7 1.0 %copy.7 = f32[2,8,32,128]{3,2,1,0:T(8,128)S(1)} copy(f32[2,8,32,128]{3,1,2,0:T(8,128)} %bitcast.16) | data formatting | bytes 524288
  31.7 0.0 copy-done.1
  31.7 0.0 copy-done.22
  31.8 0.0 copy-start.3
  31.8 1.6 %copy-done.3 = f32[4096,128]{1,0:T(8,128)S(1)} copy-done((f32[4096,128]{1,0:T(8,128)S(1)}, f32[4096,128]{1,0:T(8,128)}, u32[]{:S(2)}) %copy-start.3) | copy-done | bytes 2097176
  33.4 0.0 copy-start.14
  33.4 0.0 copy-start.16
  33.4 3.8 %early.1 = (f32[2048,128]{1,0:T(8,128)S(1)}, bf16[2,12288]{1,0:T(2,128)(2,1)S(1)}) custom-call(bf16[128,12288]{1,0:T(8,128)(2,1)S(1)} %copy-done.1, f32[4096,128]{1,0:T(8,128)S(1)} %copy-done.3, f32[16,32,128]{2,1,0:T(8,128)S(1)} %bitcast.12, f32[16,32,128]{2,1,0:T(8,128)S(1)} %bitcast.14, f32[32,128]{1,0:T(8,128)S(1)} %bitcast.18), custom_call_target="tpu_custom_call" | custom-call | flops 16777216 | bytes 2097152 | tf_op jit(solution)/shard_map/early/pallas_call | solution.py:302
  37.2 0.0 copy-start.10
  37.2 1.0 %copy-done.10 = f32[2048,128]{1,0:T(8,128)} copy-done((f32[2048,128]{1,0:T(8,128)}, f32[2048,128]{1,0:T(8,128)S(1)}, u32[]{:S(2)}) %copy-start.10) | copy-done | bytes 1048600
  38.2 3.4 %collective-permute-start = (bf16[2,12288]{1,0:T(2,128)(2,1)S(1)}, bf16[2,12288]{1,0:T(2,128)(2,1)S(1)}, u32[]{:S(2)}, u32[]{:S(2)}) collective-permute-start(bf16[2,12288]{1,0:T(2,128)(2,1)S(1)} %get-tuple-element.17), channel_id=1, source_target_pairs={{0,1},{1,2},{2,3},{3,4},{4,5},{5,6},{6,7},{7,8},{8,9},{9,10},{10,1... | collective-permute-start | bytes 147464 | tf_op jit(solution)/shard_map/ppermute | solution.py:315
  41.6 5.6 %collective-permute-done.halo_ref = bf16[2,12288]{1,0:T(2,128)(2,1)S(1)} collective-permute-done((bf16[2,12288]{1,0:T(2,128)(2,1)S(1)}, bf16[2,12288]{1,0:T(2,128)(2,1)S(1)}, u32[]{:S(2)}, u32[]{:S(2)}) %collective-permute-start) | collective-permute-done | bytes 49184 | tf_op jit(solution)/shard_map/ppermute | solution.py:315
  47.2 0.0 copy-done.14
  47.2 0.0 copy-done.16
  47.2 5.6 %late.1 = (f32[2048,128]{1,0:T(8,128)S(1)}, f32[4096,128]{1,0:T(8,128)S(1)}, f32[32,16,8,128]{3,2,1,0:T(8,128)S(1)}, f32[32,16,128]{2,1,0:T(8,128)S(1)}, f32[32,8,128]{2,1,0:T(8,128)S(1)}) custom-call(bf16[128,12288]{1,0:T(8,128)(2,1)S(1)} %copy-done.1, bf16[2,12288]{1,0:T(2,128)(2,1)S(1)} %collective-permute-done.halo_ref, ...), custom_call_target="tpu_custom_call" | custom-call | flops 16777216 | bytes 2097152 | tf_op jit(solution)/shard_map/late/pallas_call | solution.py:318
  52.8 0.0 copy-start.6
  52.8 1.3 %copy-done.6 = f32[4096,128]{1,0:T(8,128)} copy-done((f32[4096,128]{1,0:T(8,128)}, f32[4096,128]{1,0:T(8,128)S(1)}, u32[]{:S(2)}) %copy-start.6) | copy-done | bytes 2097176
  54.1 0.0 copy-start.8
  54.1 1.3 %copy-done.8 = f32[32,16,8,128]{3,2,1,0:T(8,128)} copy-done((f32[32,16,8,128]{3,2,1,0:T(8,128)}, f32[32,16,8,128]{3,2,1,0:T(8,128)S(1)}, u32[]{:S(2)}) %copy-start.8) | copy-done | bytes 2097176
  55.5 0.0 copy-start.12
  55.5 1.0 %copy-done.12 = f32[2048,128]{1,0:T(8,128)} copy-done((f32[2048,128]{1,0:T(8,128)}, f32[2048,128]{1,0:T(8,128)S(1)}, u32[]{:S(2)}) %copy-start.12) | copy-done | bytes 1048600
  56.5 0.0 copy-start.17
  56.5 0.7 %copy-done.17 = f32[32,16,128]{2,1,0:T(8,128)} copy-done((f32[32,16,128]{2,1,0:T(8,128)}, f32[32,16,128]{2,1,0:T(8,128)S(1)}, u32[]{:S(2)}) %copy-start.17) | copy-done | bytes 262168
  57.2 0.0 copy-start.20
  57.2 0.6 copy-done.20
  57.8 0.0 all-to-all-done.1.carry_ref
  57.8 0.0 copy-start.7
  57.8 1.6 %copy-done.7 = f32[4096,128]{1,0:T(8,128)S(1)} copy-done((f32[4096,128]{1,0:T(8,128)S(1)}, f32[4096,128]{1,0:T(8,128)}, u32[]{:S(2)}) %copy-start.7) | copy-done | bytes 2097176
  59.4 0.0 copy-start.9
  59.4 1.6 %copy-done.9 = f32[32,16,8,128]{3,2,1,0:T(8,128)S(1)} copy-done((f32[32,16,8,128]{3,2,1,0:T(8,128)S(1)}, f32[32,16,8,128]{3,2,1,0:T(8,128)}, u32[]{:S(2)}) %copy-start.9) | copy-done | bytes 2097176
  61.0 0.0 copy-start.11
  61.0 1.2 %copy-done.11 = f32[2048,128]{1,0:T(8,128)S(1)} copy-done((f32[2048,128]{1,0:T(8,128)S(1)}, f32[2048,128]{1,0:T(8,128)}, u32[]{:S(2)}) %copy-start.11) | copy-done | bytes 1048600
  62.2 0.0 copy-start.13
  62.2 1.2 %copy-done.13 = f32[2048,128]{1,0:T(8,128)S(1)} copy-done((f32[2048,128]{1,0:T(8,128)S(1)}, f32[2048,128]{1,0:T(8,128)}, u32[]{:S(2)}) %copy-start.13) | copy-done | bytes 1048600
  63.5 0.0 copy-start.18
  63.5 0.9 %copy-done.18 = f32[32,16,128]{2,1,0:T(8,128)S(1)} copy-done((f32[32,16,128]{2,1,0:T(8,128)S(1)}, f32[32,16,128]{2,1,0:T(8,128)}, u32[]{:S(2)}) %copy-start.18) | copy-done | bytes 262168
  64.4 0.0 copy-start.21
  64.4 0.9 %copy-done.21 = f32[32,8,128]{2,1,0:T(8,128)S(1)} copy-done((f32[32,8,128]{2,1,0:T(8,128)S(1)}, f32[32,8,128]{2,1,0:T(8,128)}, u32[]{:S(2)}) %copy-start.21) | copy-done | bytes 131096
  65.3 3.4 %final.1 = bf16[128,4096]{1,0:T(8,128)(2,1)} custom-call(bf16[32,16,128]{2,1,0:T(8,128)(2,1)S(1)} %all-to-all-done.1.carry_ref, f32[2048,128]{1,0:T(8,128)S(1)} %copy-done.11, f32[2048,128]{1,0:T(8,128)S(1)} %copy-done.13, f32[4096,128]{1,0:T(8,128)S(1)} %copy-done.7, f32[32,16,8,128]{3,2,1,0:T(8,128)S(1)} %copy-done.9, f32[32,16,128]{2,1,0:T(8,128)S(1)} %copy-done.18, ...), custom_call_target="tpu_custom_call" | custom-call | tf_op jit(solution)/shard_map/final/pallas_call | solution.py:340
  (1 shorter events, 0.0 us)
Async XLA Ops:
  0.0 1.9 %copy-start = (bf16[128,12288]{1,0:T(8,128)(2,1)S(1)}, bf16[128,12288]{1,0:T(8,128)(2,1)}, u32[]{:S(2)}) copy-start(bf16[128,12288]{1,0:T(8,128)(2,1)} %proj_ref.5) | copy-start | bytes 9437188
  1.9 0.9 %copy-start.4 = (f32[4096,16]{0,1:T(8,128)S(1)}, f32[4096,16]{0,1:T(8,128)}, u32[]{:S(2)}) copy-start(f32[4096,16]{0,1:T(8,128)} %param.7) | copy-start | bytes 786436
  2.8 0.9 %copy-start.15 = (f32[3,12288]{1,0:T(4,128)S(1)}, f32[3,12288]{1,0:T(4,128)}, u32[]{:S(2)}) copy-start(f32[3,12288]{1,0:T(4,128)} %taps_ref.1) | copy-start | bytes 442372
  3.8 14.0 %copy-start.5 = (f32[4096,16]{0,1:T(8,128)S(1)}, f32[4096,16]{0,1:T(8,128)}, u32[]{:S(2)}) copy-start(f32[4096,16]{0,1:T(8,128)} %param.7) | copy-start | bytes 786436
  3.8 28.0 %copy-start.1 = (bf16[128,12288]{1,0:T(8,128)(2,1)S(1)}, bf16[128,12288]{1,0:T(8,128)(2,1)}, u32[]{:S(2)}) copy-start(bf16[128,12288]{1,0:T(8,128)(2,1)} %proj_ref.5) | copy-start | bytes 9437188
  3.8 28.0 %copy-start.22 = (f32[4096]{0:T(1024)S(1)}, f32[4096]{0:T(1024)}, u32[]{:S(2)}) copy-start(f32[4096]{0:T(1024)} %param.9) | copy-start | bytes 49156
  8.8 1.3 %copy-start.2 = (f32[4096,128]{1,0:T(8,128)}, f32[4096,128]{1,0:T(8,128)S(1)}, u32[]{:S(2)}) copy-start(f32[4096,128]{1,0:T(8,128)S(1)} %get-tuple-element.15.mixed_ref) | copy-start | bytes 6291460
  10.2 0.7 copy-start.19
  10.9 14.7 %all-to-all-start = ((bf16[32,24,128]{2,1,0:T(8,128)(2,1)}), bf16[32,24,128]{2,1,0:T(8,128)(2,1)}, u32[]{:S(2)}, u32[]{:S(2)}) async-start(bf16[32,24,128]{2,1,0:T(8,128)(2,1)} %copy-done.19), calls=%async_computation | async-start | bytes 393216 | tf_op jit(solution)/shard_map/all_to_all | solution.py:271
  27.4 30.5 %all-to-all-start.1 = ((bf16[32,16,128]{2,1,0:T(8,128)(2,1)}), bf16[32,16,128]{2,1,0:T(8,128)(2,1)S(1)}, u32[]{:S(2)}, u32[]{:S(2)}) async-start(bf16[32,16,128]{2,1,0:T(8,128)(2,1)} %scan.1.after_ref), calls=%async_computation.1 | async-start | bytes 262144 | tf_op jit(solution)/shard_map/all_to_all | solution.py:271
  31.8 1.6 %copy-start.3 = (f32[4096,128]{1,0:T(8,128)S(1)}, f32[4096,128]{1,0:T(8,128)}, u32[]{:S(2)}) copy-start(f32[4096,128]{1,0:T(8,128)} %copy-done.2) | copy-start | bytes 6291460
  33.4 13.8 %copy-start.14 = (f32[4096,16]{0,1:T(8,128)S(1)}, f32[4096,16]{0,1:T(8,128)}, u32[]{:S(2)}) copy-start(f32[4096,16]{0,1:T(8,128)} %param.8) | copy-start | bytes 786436
  33.4 13.8 %copy-start.16 = (f32[3,12288]{1,0:T(4,128)S(1)}, f32[3,12288]{1,0:T(4,128)}, u32[]{:S(2)}) copy-start(f32[3,12288]{1,0:T(4,128)} %taps_ref.1) | copy-start | bytes 442372
  37.2 1.0 %copy-start.10 = (f32[2048,128]{1,0:T(8,128)}, f32[2048,128]{1,0:T(8,128)S(1)}, u32[]{:S(2)}) copy-start(f32[2048,128]{1,0:T(8,128)S(1)} %get-tuple-element.16.early_ref) | copy-start | bytes 3145732
  38.2 9.0 %collective-permute-start = (bf16[2,12288]{1,0:T(2,128)(2,1)S(1)}, bf16[2,12288]{1,0:T(2,128)(2,1)S(1)}, u32[]{:S(2)}, u32[]{:S(2)}) collective-permute-start(bf16[2,12288]{1,0:T(2,128)(2,1)S(1)} %get-tuple-element.17), channel_id=1, source_target_pairs={{0,1},{1,2},{2,3},{3,4},{4,5},{5,6},{6,7},{7,8},{8,9},{9,10},{10,1... | collective-permute-start | bytes 147464 | tf_op jit(solution)/shard_map/ppermute | solution.py:315
  52.8 1.3 %copy-start.6 = (f32[4096,128]{1,0:T(8,128)}, f32[4096,128]{1,0:T(8,128)S(1)}, u32[]{:S(2)}) copy-start(f32[4096,128]{1,0:T(8,128)S(1)} %get-tuple-element.19.query_ref) | copy-start | bytes 6291460
  54.1 1.3 %copy-start.8 = (f32[32,16,8,128]{3,2,1,0:T(8,128)}, f32[32,16,8,128]{3,2,1,0:T(8,128)S(1)}, u32[]{:S(2)}) copy-start(f32[32,16,8,128]{3,2,1,0:T(8,128)S(1)} %get-tuple-element.20.start_ref) | copy-start | bytes 6291460
  55.5 1.0 %copy-start.12 = (f32[2048,128]{1,0:T(8,128)}, f32[2048,128]{1,0:T(8,128)S(1)}, u32[]{:S(2)}) copy-start(f32[2048,128]{1,0:T(8,128)S(1)} %get-tuple-element.18.late_ref) | copy-start | bytes 3145732
  56.5 0.7 %copy-start.17 = (f32[32,16,128]{2,1,0:T(8,128)}, f32[32,16,128]{2,1,0:T(8,128)S(1)}, u32[]{:S(2)}) copy-start(f32[32,16,128]{2,1,0:T(8,128)S(1)} %get-tuple-element.21.stride_ref) | copy-start | bytes 786436
  57.2 0.7 copy-start.20
  57.8 1.6 %copy-start.7 = (f32[4096,128]{1,0:T(8,128)S(1)}, f32[4096,128]{1,0:T(8,128)}, u32[]{:S(2)}) copy-start(f32[4096,128]{1,0:T(8,128)} %copy-done.6) | copy-start | bytes 6291460
  59.4 1.6 %copy-start.9 = (f32[32,16,8,128]{3,2,1,0:T(8,128)S(1)}, f32[32,16,8,128]{3,2,1,0:T(8,128)}, u32[]{:S(2)}) copy-start(f32[32,16,8,128]{3,2,1,0:T(8,128)} %copy-done.8) | copy-start | bytes 6291460
  61.0 1.2 %copy-start.11 = (f32[2048,128]{1,0:T(8,128)S(1)}, f32[2048,128]{1,0:T(8,128)}, u32[]{:S(2)}) copy-start(f32[2048,128]{1,0:T(8,128)} %copy-done.10) | copy-start | bytes 3145732
  62.2 1.2 %copy-start.13 = (f32[2048,128]{1,0:T(8,128)S(1)}, f32[2048,128]{1,0:T(8,128)}, u32[]{:S(2)}) copy-start(f32[2048,128]{1,0:T(8,128)} %copy-done.12) | copy-start | bytes 3145732
  63.5 0.9 %copy-start.18 = (f32[32,16,128]{2,1,0:T(8,128)S(1)}, f32[32,16,128]{2,1,0:T(8,128)}, u32[]{:S(2)}) copy-start(f32[32,16,128]{2,1,0:T(8,128)} %copy-done.17) | copy-start | bytes 786436
  64.4 0.9 %copy-start.21 = (f32[32,8,128]{2,1,0:T(8,128)S(1)}, f32[32,8,128]{2,1,0:T(8,128)}, u32[]{:S(2)}) copy-start(f32[32,8,128]{2,1,0:T(8,128)} %copy-done.20) | copy-start | bytes 393220

commit v3 on v2

v3 whole, which is shorter than its diff:
```python
import functools

import jax
import jax.numpy as jnp
from jax import lax
from jax.experimental import pallas as pl
from jax.experimental.pallas import tpu as pltpu
from jax.sharding import PartitionSpec as P

LANES = 128
SUB = 8
PIECES = 4
AXES = ("outer", "inner")
F32 = jnp.float32
BF16 = jnp.bfloat16
HBM = pl.BlockSpec(memory_space=pltpu.HBM)
VMEM = pl.BlockSpec(memory_space=pltpu.VMEM)
PARAMS = pltpu.CompilerParams(vmem_limit_bytes=32 * 1024 * 1024)


def held(x):
    return pltpu.with_memory_space_constraint(x, pltpu.VMEM)


def pinned(x):
    return pltpu.with_memory_space_constraint(x, pltpu.HBM)


def column(group):
    return pl.ds(pl.multiple_of(group * LANES, LANES), LANES)


def tree_sum(terms):
    while len(terms) > 1:
        terms = [a + b for a, b in zip(terms[::2], terms[1::2])] + ([terms[-1]] if len(terms) % 2 else [])
    return terms[0]


def short_filter(pad_ref, taps, rows):
    return (
        taps[0:1] * pad_ref[SUB : SUB + rows, :]
        + taps[1:2] * pad_ref[SUB - 1 : SUB - 1 + rows, :]
        + taps[2:3] * pad_ref[SUB - 2 : SUB - 2 + rows, :]
    )


def sublane():
    return lax.broadcasted_iota(jnp.int32, (SUB, LANES), 0)


def state_kernel(proj_ref, taps_hbm, rates_hbm, sent_hbm, mixed_hbm, k_buf, v_buf, taps_ref, rates_ref, table, ends, pad_k, pad_v, sent_ref, mixed_ref, sems, more,
):
    rows, channels = k_buf.shape
    modes = rates_ref.shape[0]
    groups = channels // LANES
    wide = channels // PIECES
    whole = [pltpu.make_async_copy(rates_hbm, rates_ref, more.at[0]), pltpu.make_async_copy(taps_hbm, taps_ref, more.at[1])]
    pieces = []
    for piece in range(PIECES):
        at = pl.ds(piece * wide, wide)
        pieces.append([
            pltpu.make_async_copy(proj_ref.at[:, pl.ds(channels + piece * wide, wide)], k_buf.at[:, at], sems.at[0, piece]),
            pltpu.make_async_copy(proj_ref.at[:, pl.ds(2 * channels + piece * wide, wide)], v_buf.at[:, at], sems.at[1, piece]),
        ])
    for copy in whole + [c for pair in pieces for c in pair]:
        copy.start()
    whole[0].wait()
    decay = jnp.exp(-rates_ref[...])
    for power in range(4):
        table[power] = decay
        decay = decay * decay
    whole[1].wait()
    row = sublane()
    leaving = []
    for piece in range(PIECES):
        for copy in pieces[piece]:
            copy.wait()

        @pl.loop(piece * (groups // PIECES), (piece + 1) * (groups // PIECES))
        def _(group):
            cols = column(group)
            pad_k[SUB : SUB + rows, :] = k_buf[:, cols].astype(F32)
            pad_v[SUB : SUB + rows, :] = v_buf[:, cols].astype(F32)
            mixed = short_filter(pad_k, taps_ref[:, column(groups + group)], rows) * short_filter(
                pad_v, taps_ref[:, column(2 * groups + group)], rows
            )
            tiles = [mixed[i * SUB : (i + 1) * SUB] for i in range(rows // SUB)]
            tiles[0] = jnp.where(row < 2, 0.0, tiles[0])
            for i, tile in enumerate(tiles):
                mixed_ref[pl.ds(pl.multiple_of(group * rows + i * SUB, SUB), SUB), :] = tile
            for mode in range(modes):
                one, two, four, eight = (
                    jnp.broadcast_to(table[power, mode : mode + 1, cols], (SUB, LANES)) for power in range(4)
                )
                total = tiles[0]
                for tile in tiles[1:]:
                    total = total * eight + tile
                total = total + four * pltpu.roll(total, 4, 0)
                total = total + two * pltpu.roll(total, 2, 0)
                total = total + one * pltpu.roll(total, 1, 0)
                ends[mode : mode + 1, :] = total[SUB - 1 :]
            first_k, first_v = pad_k[SUB : 2 * SUB, :], pad_v[SUB : 2 * SUB, :]
            last_k, last_v = pad_k[rows : SUB + rows, :], pad_v[rows : SUB + rows, :]
            ends[modes:, :] = jnp.where(
                row < 2,
                first_k,
                jnp.where(row < 4, pltpu.roll(first_v, 2, 0), jnp.where(row < 6, pltpu.roll(last_k, 6, 0), last_v)),
            )
            sent_ref[group] = ends[...].astype(BF16)

        share = groups // PIECES
        at = pl.ds(piece * share * rows, share * rows)
        leaving.append(pltpu.make_async_copy(mixed_ref.at[at], mixed_hbm.at[at], sems.at[2, piece]))
        at = pl.ds(piece * share, share)
        leaving.append(pltpu.make_async_copy(sent_ref.at[at], sent_hbm.at[at], sems.at[3, piece]))
        for copy in leaving[-2:]:
            copy.start()
    for copy in leaving:
        copy.wait()


def scan_kernel(rows, modes, got_ref, rates_ref, tk_ref, tv_ref, after_ref, out_ref):
    one = jnp.exp(-rates_ref[...])
    two = jnp.exp(-2.0 * rates_ref[...])
    rest = jnp.exp(-(rows - 2.0) * rates_ref[...])
    row = sublane()
    taps = [jnp.where(row < 2, tk_ref[i : i + 1, :], tv_ref[i : i + 1, :]) for i in range(3)]

    def step(place, carry):
        state, before = carry
        edge = got_ref[place, modes:, :].astype(F32)
        feat = (
            taps[0] * edge
            + taps[1] * jnp.where(row % 2 == 1, pltpu.roll(edge, 1, 0), pltpu.roll(before, 3, 0))
            + taps[2] * pltpu.roll(before, 4, 0)
        )
        mixed = feat * pltpu.roll(feat, SUB - 2, 0)
        state = state * two + one * mixed[0:1] + mixed[1:2]
        out_ref[place] = state.astype(BF16)
        return state * rest + got_ref[place, :modes, :].astype(F32), edge

    first = (jnp.zeros((modes, LANES), F32), jnp.zeros((SUB, LANES), F32))
    lax.fori_loop(0, got_ref.shape[0], step, first, unroll=8)


def recur(rows, blocks, mixed_ref, decay_ref, gain_ref, skip_ref, out_ref, before, after):
    modes = decay_ref.shape[0] // (blocks * SUB)
    for block in range(blocks):
        before[block].wait()
        at = [pl.ds((m * blocks + block) * SUB, SUB) for m in range(modes)]
        decays = [decay_ref[a, :] for a in at]
        gains = [gain_ref[a, :] for a in at]
        skip = skip_ref[pl.ds(block * SUB, SUB), :]

        def step(token, states):
            here = pl.ds(block * SUB * rows + token, SUB, stride=rows)
            x = mixed_ref[here, :]
            states = tuple(s * d + x for s, d in zip(states, decays))
            out_ref[here, :] = tree_sum([s * g for s, g in zip(states, gains)] + [skip * x])
            return states

        lax.fori_loop(0, rows, step, tuple(jnp.zeros((SUB, LANES), F32) for _ in range(modes)), unroll=4)
        after[block].start()


def spread(rates_ref, residues_ref, decay_ref, gain_ref, first, groups):
    modes = rates_ref.shape[0]
    for group in range(groups):
        cols = slice((first + group) * LANES, (first + group + 1) * LANES)
        rates = rates_ref[:, cols]
        at = pl.ds(group, modes, stride=groups)
        decay_ref[at, :] = jnp.exp(-rates)
        gain_ref[at, :] = residues_ref[:, cols] * jnp.sqrt(2.0 * rates)


def block_copies(blocks, size, first, from_ref, to_ref, sems):
    copies = []
    for block in range(blocks):
        source = from_ref.at[pl.ds((first + block) * size, size)]
        copies.append(pltpu.make_async_copy(source, to_ref.at[pl.ds(block * size, size)], sems.at[block]))
    return copies


def early_kernel(
    blocks, proj_ref, mixed_hbm, rates_hbm, residues_hbm, skip_hbm, out_hbm, tail_ref,
    buf, mixed_ref, rates_ref, residues_ref, skip_ref, decay_ref, gain_ref, out_ref, sems, in_sems, out_sems,
):
    rows = proj_ref.shape[0]
    copies = [
        pltpu.make_async_copy(rates_hbm, rates_ref, sems.at[0]),
        pltpu.make_async_copy(residues_hbm, residues_ref, sems.at[1]),
        pltpu.make_async_copy(skip_hbm, skip_ref, sems.at[2]),
        pltpu.make_async_copy(proj_ref.at[pl.ds(rows - 2 * SUB, 2 * SUB), :], buf, sems.at[3]),
    ]
    size = SUB * rows
    before = block_copies(blocks, size, 0, mixed_hbm, mixed_ref, in_sems)
    after = block_copies(blocks, size, 0, out_ref, out_hbm, out_sems)
    for copy in copies + before:
        copy.start()
    for copy in copies:
        copy.wait()
    tail_ref[...] = buf[2 * SUB - 2 :, :]
    spread(rates_ref, residues_ref, decay_ref, gain_ref, 0, blocks * SUB)
    recur(rows, blocks, mixed_ref, decay_ref, gain_ref, skip_ref, out_ref, before, after)
    for copy in after:
        copy.wait()


def late_kernel(
    first, blocks, proj_ref, halo_ref, after_ref, mixed_hbm, rates_hbm, residues_hbm, skip_hbm, taps_hbm,
    out_hbm, query_hbm, start_hbm, stride_hbm, edge_hbm,
    q_buf, head_buf, pad, mixed_ref, rates_ref, residues_ref, skip_ref, taps_ref, decay_ref, gain_ref,
    out_ref, query_ref, start_ref, stride_ref, edge_ref, sems, in_sems, out_sems,
):
    rows, channels = q_buf.shape
    modes = rates_ref.shape[0]
    groups = channels // LANES
    copies = [
        pltpu.make_async_copy(rates_hbm, rates_ref, sems.at[0]),
        pltpu.make_async_copy(residues_hbm, residues_ref, sems.at[1]),
        pltpu.make_async_copy(skip_hbm, skip_ref, sems.at[2]),
        pltpu.make_async_copy(taps_hbm, taps_ref, sems.at[3]),
        pltpu.make_async_copy(proj_ref.at[:, pl.ds(0, channels)], q_buf, sems.at[4]),
        pltpu.make_async_copy(proj_ref.at[pl.ds(0, 2 * SUB), pl.ds(channels, 2 * channels)], head_buf, sems.at[5]),
    ]
    size = SUB * rows
    before = block_copies(blocks, size, first, mixed_hbm, mixed_ref, in_sems)
    after = block_copies(blocks, size, 0, out_ref, out_hbm, out_sems)
    for copy in copies + before:
        copy.start()
    for copy in copies:
        copy.wait()
    row = sublane()
    place = row.astype(F32) - 1.0

    @pl.loop(0, groups)
    def _(group):
        cols = column(group)
        pad[SUB - 2 : SUB, :] = halo_ref[:, cols].astype(F32)
        pad[SUB : SUB + rows, :] = q_buf[:, cols].astype(F32)
        query_ref[pl.ds(pl.multiple_of(group * rows, rows), rows), :] = short_filter(pad, taps_ref[:, cols], rows)
        rates = rates_ref[:, cols]
        gains = residues_ref[:, cols] * jnp.sqrt(2.0 * rates)
        stride_ref[group] = jnp.exp(-SUB * rates)
        starts = [jnp.exp(-rates[m : m + 1] * place) * gains[m : m + 1] for m in range(modes)]
        for mode in range(modes):
            start_ref[group, mode] = starts[mode]
        mixed = None
        for which in (1, 2):
            at = column(which * groups + group)
            pad[SUB - 2 : SUB, :] = halo_ref[:, at].astype(F32)
            pad[SUB : 3 * SUB, :] = head_buf[:, column((which - 1) * groups + group)].astype(F32)
            feat = short_filter(pad, taps_ref[:, at], SUB)
            mixed = feat if mixed is None else mixed * feat
        skip = skip_ref[pl.ds(group, 1), :]
        own = skip * mixed - jnp.where(row == 0, tree_sum(starts) * pltpu.roll(mixed, SUB - 1, 0), 0.0)
        edge_ref[group] = jnp.where(row < 2, own, 0.0)

    leaving = [
        pltpu.make_async_copy(query_ref, query_hbm, sems.at[6]),
        pltpu.make_async_copy(start_ref, start_hbm, sems.at[7]),
        pltpu.make_async_copy(stride_ref, stride_hbm, sems.at[8]),
        pltpu.make_async_copy(edge_ref, edge_hbm, sems.at[9]),
    ]
    for copy in leaving:
        copy.start()
    spread(rates_ref, residues_ref, decay_ref, gain_ref, first * SUB, blocks * SUB)
    recur(rows, blocks, mixed_ref, decay_ref, gain_ref, skip_ref.at[pl.ds(first * SUB, blocks * SUB)], out_ref, before, after)
    for copy in leaving + after:
        copy.wait()


def final_kernel(
    carry_ref, early_hbm, late_hbm, query_hbm, start_hbm, stride_hbm, edge_hbm, out_hbm,
    local_ref, query_ref, start_ref, stride_ref, edge_ref, out_buf, sems,
):
    rows, channels = out_buf.shape
    groups, modes = stride_ref.shape[0], stride_ref.shape[1]
    split = early_hbm.shape[0] // rows
    share = groups // PIECES
    arriving = []
    for piece in range(PIECES):
        low = piece * share
        local_hbm, base = (early_hbm, 0) if low + share <= split else (late_hbm, split)
        by_row = pl.ds(low * rows, share * rows)
        by_group = pl.ds(low, share)
        arriving.append([
            pltpu.make_async_copy(start_hbm.at[by_group], start_ref.at[by_group], sems.at[piece, 0]),
            pltpu.make_async_copy(stride_hbm.at[by_group], stride_ref.at[by_group], sems.at[piece, 1]),
            pltpu.make_async_copy(edge_hbm.at[by_group], edge_ref.at[by_group], sems.at[piece, 2]),
            pltpu.make_async_copy(local_hbm.at[pl.ds((low - base) * rows, share * rows)], local_ref.at[by_row], sems.at[piece, 3]),
            pltpu.make_async_copy(query_hbm.at[by_row], query_ref.at[by_row], sems.at[piece, 4]),
        ])
        for copy in arriving[-1]:
            copy.start()
    copies = []
    for piece in range(PIECES):
        low = piece * share
        for copy in arriving[piece]:
            copy.wait()

        @pl.loop(low, low + share)
        def _(group):
            carry = carry_ref[group].astype(F32)
            strides = [jnp.broadcast_to(stride_ref[group, m : m + 1, :], (SUB, LANES)) for m in range(modes)]
            terms = [start_ref[group, m] * carry[m : m + 1] for m in range(modes)]
            made = []
            for tile in range(rows // SUB):
                at = pl.ds(pl.multiple_of(group * rows + tile * SUB, SUB), SUB)
                own = local_ref[at, :]
                if tile == 0:
                    own = own + edge_ref[group]
                made.append(query_ref[at, :] * (tree_sum(terms) + own))
                if tile + 1 < rows // SUB:
                    terms = [t * s for t, s in zip(terms, strides)]
            for i in range(0, len(made), 2):
                out_buf[i * SUB : (i + 2) * SUB, column(group)] = jnp.concatenate(made[i : i + 2], 0).astype(BF16)

        at = pl.ds(low * LANES, share * LANES)
        copies.append(pltpu.make_async_copy(out_buf.at[:, at], out_hbm.at[:, at], sems.at[piece, 5]))
        copies[-1].start()
    for copy in copies:
        copy.wait()


def on_device(projected, short_taps, rates, residues, skip_gain):
    rows, feature_width = projected.shape
    channels = feature_width // 3
    modes = rates.shape[1]
    groups = channels // LANES
    count = lax.axis_size(AXES)
    place = lax.axis_index(AXES)
    own = channels // count
    rates_t, residues_t = rates.T, residues.T
    sent_rows = modes + SUB
    dma = pltpu.SemaphoreType.DMA

    def f32_vmem(*shape):
        return pltpu.VMEM(shape, F32)

    sent, mixed = pl.pallas_call(
        state_kernel,
        in_specs=[HBM, HBM, HBM],
        out_specs=[HBM, HBM],
        out_shape=[pltpu.HBM((groups, sent_rows, LANES), BF16), pltpu.HBM((groups * rows, LANES), F32)],
        scratch_shapes=[
            pltpu.VMEM((rows, channels), BF16),
            pltpu.VMEM((rows, channels), BF16),
            f32_vmem(*short_taps.shape),
            f32_vmem(modes, channels),
            f32_vmem(4, modes, channels),
            f32_vmem(sent_rows, LANES),
            f32_vmem(rows + SUB, LANES),
            f32_vmem(rows + SUB, LANES),
            pltpu.VMEM((groups, sent_rows, LANES), BF16),
            f32_vmem(groups * rows, LANES),
            dma((4, PIECES)),
            dma((2,)),
        ],
        compiler_params=PARAMS,
        name="state",
    )(pinned(projected), pinned(short_taps), pinned(rates_t))

    def exchange(x):
        return lax.all_to_all(x, AXES, split_axis=0, concat_axis=0, tiled=True)

    if own == LANES:
        got = exchange(sent)
    else:
        parts = sent.reshape(groups, sent_rows, LANES // own, own).transpose(0, 2, 1, 3)
        got = exchange(parts.reshape(count, sent_rows, own))
        got = jnp.pad(got, ((0, 0), (0, 0), (0, LANES - own)))

    def own_part(x, start=0):
        part = lax.dynamic_slice_in_dim(x, start + place * own, own, 1)
        return part if own == LANES else jnp.pad(part, ((0, 0), (0, LANES - own)))

    blocks = groups // SUB
    early_blocks = blocks // 2
    late_blocks = blocks - early_blocks
    skip = skip_gain.reshape(groups, LANES)
    cost = pl.CostEstimate(flops=2 * modes * rows * channels, bytes_accessed=4 * rows * channels, transcendentals=0)

    def recur_scratch(count):
        return [
            f32_vmem(modes, channels),
            f32_vmem(modes, channels),
            f32_vmem(groups, LANES),
        ], [
            f32_vmem(count * SUB * modes, LANES),
            f32_vmem(count * SUB * modes, LANES),
            f32_vmem(count * SUB * rows, LANES),
        ]

    params, tables = recur_scratch(early_blocks)
    early, tail = pl.pallas_call(
        functools.partial(early_kernel, early_blocks),
        in_specs=[HBM] * 5,
        out_specs=[HBM, VMEM],
        out_shape=[pltpu.HBM((early_blocks * SUB * rows, LANES), F32), pltpu.VMEM((2, feature_width), BF16)],
        scratch_shapes=[
            pltpu.VMEM((2 * SUB, feature_width), BF16),
            f32_vmem(early_blocks * SUB * rows, LANES),
            *params,
            *tables,
            dma((4,)),
            dma((early_blocks,)),
            dma((early_blocks,)),
        ],
        cost_estimate=cost,
        compiler_params=PARAMS,
        name="early",
    )(pinned(projected), pinned(mixed), pinned(rates_t), pinned(residues_t), pinned(skip))
    halo = lax.ppermute(tail, AXES, [(s, s + 1) for s in range(count - 1)])

    scanned = pl.pallas_call(
        functools.partial(scan_kernel, rows, modes),
        in_specs=[VMEM] * 4 + [HBM],
        out_specs=VMEM,
        out_shape=pltpu.VMEM((count, modes, LANES), BF16),
        compiler_params=PARAMS,
        name="scan",
    )(held(got), own_part(rates_t), own_part(short_taps, channels), own_part(short_taps, 2 * channels), pinned(early))
    if own == LANES:
        carry = exchange(scanned)
    else:
        parts = exchange(scanned[:, :, :own]).reshape(groups, LANES // own, modes, own)
        carry = parts.transpose(0, 2, 1, 3).reshape(groups, modes, LANES)

    params, tables = recur_scratch(late_blocks)
    made = [(groups * rows, LANES), (groups, modes, SUB, LANES), (groups, modes, LANES), (groups, SUB, LANES)]
    late, query, start, stride, edge = pl.pallas_call(
        functools.partial(late_kernel, early_blocks, late_blocks),
        in_specs=[HBM, VMEM] + [HBM] * 6,
        out_specs=[HBM] * 5,
        out_shape=[pltpu.HBM((late_blocks * SUB * rows, LANES), F32)] + [pltpu.HBM(shape, F32) for shape in made],
        scratch_shapes=[
            pltpu.VMEM((rows, channels), BF16),
            pltpu.VMEM((2 * SUB, 2 * channels), BF16),
            f32_vmem(rows + SUB, LANES),
            f32_vmem(late_blocks * SUB * rows, LANES),
            *params,
            f32_vmem(*short_taps.shape),
            *tables,
            *[f32_vmem(*shape) for shape in made],
            dma((10,)),
            dma((late_blocks,)),
            dma((late_blocks,)),
        ],
        cost_estimate=cost,
        compiler_params=PARAMS,
        name="late",
    )(pinned(projected), held(halo), pinned(scanned), pinned(mixed), pinned(rates_t), pinned(residues_t), pinned(skip), pinned(short_taps))

    return pl.pallas_call(
        final_kernel,
        in_specs=[VMEM] + [HBM] * 6,
        out_specs=HBM,
        out_shape=pltpu.HBM((rows, channels), BF16),
        scratch_shapes=[f32_vmem(groups * rows, LANES), *[f32_vmem(*shape) for shape in made], pltpu.VMEM((rows, channels), BF16), dma((PIECES, 6))],
        compiler_params=PARAMS,
        name="final",
    )(held(carry), pinned(early), pinned(late), pinned(query), pinned(start), pinned(stride), pinned(edge))


def solution(mesh):
    in_specs = (P(AXES, None), P(), P(), P(), P())
    out_specs = P(AXES, None)
    return jax.shard_map(
        on_device, mesh=mesh, in_specs=in_specs, out_specs=out_specs, check_vma=False
    )
```

time: 69.3 us -> 49.3 us (0.71)
  local copies, waits for them, and re-layouts: 22.6 us -> 1.41 us
  Pallas kernels: 19.7 us -> 26.5 us
  waiting for transfers between devices: 13.4 us -> 7.01 us
  starting transfers between devices: 12.9 us -> 13.9 us
    unnamed x48 -> x0, local copies, waits for them, and re-layouts: 21.9 us -> none
    all_to_all x2, waiting for transfers between devices: 7.81 us -> 1.39 us  [exchange(): return lax.all_to_all(x, AXES, split_axis=0, concat_axis=0, tiled=True)]
    pallas_call x2, Pallas kernels: 8.44 us -> 11.9 us  [the longest x1 6.9 us: on_device(): pl.pallas_call(state_kernel, in_specs=[HBM, HBM, HBM], out_specs=[HBM, HB...]
    pallas_call x1, Pallas kernels: 5.62 us -> 8.05 us  [on_device(): pl.pallas_call(functools.partial(late_kernel, early_blocks, late_blocks),...]
    pallas_call x1, Pallas kernels: 3.84 us -> 5.66 us  [on_device(): pl.pallas_call(functools.partial(early_kernel, early_blocks), in_specs=[H...]
    all_to_all x2, starting transfers between devices: 9.45 us -> 10.6 us  [exchange(): return lax.all_to_all(x, AXES, split_axis=0, concat_axis=0, tiled=True)]
    pallas_call x1, Pallas kernels: 1.8 us -> 0.88 us  [on_device(): pl.pallas_call(functools.partial(scan_kernel, rows, modes), in_specs=[VME...]
    dynamic_slice x2, local copies, waits for them, and re-layouts: 0.71 us -> 1.41 us  [own_part(): part = lax.dynamic_slice_in_dim(x, start + place * own, own, 1)]
  transfers between devices with their start and end apart: 3 -> 3, of which waited for: 2 -> 2; matrix products, arithmetic and copies ran while one was open for 3% -> 3% of each run, Pallas kernels for 14% -> 28%
where the time goes in v3:
time: 49.3 us; the launch traced here: 48.9 us
  Pallas kernels  26.5 us (54%)
  starting transfers between devices  13.9 us (28%)
  waiting for transfers between devices  7.01 us (14%)
  local copies, waits for them, and re-layouts  1.41 us (3%)
    all_to_all x2, starting transfers between devices, exchange(): return lax.all_to_all(x, AXES, split_axis=0, concat_axis=0, tiled=True)  10.6 us
    pallas_call x1, Pallas kernels, on_device(): pl.pallas_call(functools.partial(late_kernel, early_blocks, late_blocks),...  8.05 us
    pallas_call x1, Pallas kernels, on_device(): pl.pallas_call(state_kernel, in_specs=[HBM, HBM, HBM], out_specs=[HBM, HB...  6.9 us
    pallas_call x1, Pallas kernels, on_device(): pl.pallas_call(functools.partial(early_kernel, early_blocks), in_specs=[H...  5.66 us
    ppermute x1, waiting for transfers between devices, on_device(): halo = lax.ppermute(tail, AXES, [(s, s + 1) for s in range(count - 1)])  5.62 us
    pallas_call x1, Pallas kernels, on_device(): pl.pallas_call(final_kernel, in_specs=[VMEM] + [HBM] * 6, out_specs=HBM,...  4.98 us
    ppermute x1, starting transfers between devices, on_device(): halo = lax.ppermute(tail, AXES, [(s, s + 1) for s in range(count - 1)])  3.38 us
    dynamic_slice x2, local copies, waits for them, and re-layouts, own_part(): part = lax.dynamic_slice_in_dim(x, start + place * own, own, 1)  1.41 us
  transfers between devices with their start and end apart: 3, of which 2 were waited for; matrix products, arithmetic and copies ran while one was open for 3% of the time, Pallas kernels for 28%

profile of v3, /device:TPU:4, one launch (start us, length us, event | category | flops | bytes accessed | tf_op | source)
XLA Modules:
  0.0 48.9 jit_solution(5256541597939792421)
XLA Ops:
  0.0 6.9 %state.1 = (bf16[32,24,128]{2,1,0:T(8,128)(2,1)}, f32[4096,128]{1,0:T(8,128)}) custom-call(bf16[128,12288]{1,0:T(8,128)(2,1)} %proj_ref.5, f32[3,12288]{1,0:T(4,128)} %taps_hbm.3, f32[16,4096]{1,0:T(8,128)} %bitcast.5), custom_call_target="tpu_custom_call" | custom-call | tf_op jit(solution)/shard_map/state/pallas_call | solution.py:341
  6.9 6.1 %all-to-all-start = ((bf16[32,24,128]{2,1,0:T(8,128)(2,1)}), bf16[32,24,128]{2,1,0:T(8,128)(2,1)S(1)}, u32[]{:S(2)}, u32[]{:S(2)}) async-start(bf16[32,24,128]{2,1,0:T(8,128)(2,1)} %get-tuple-element.14), calls=%async_computation | async-start | bytes 393216 | tf_op jit(solution)/shard_map/all_to_all | solution.py:365
  13.0 5.7 %early.1 = (f32[2048,128]{1,0:T(8,128)}, bf16[2,12288]{1,0:T(2,128)(2,1)S(1)}) custom-call(bf16[128,12288]{1,0:T(8,128)(2,1)} %proj_ref.5, f32[4096,128]{1,0:T(8,128)} %get-tuple-element.15.mixed_hbm, f32[16,4096]{1,0:T(8,128)} %bitcast.6, f32[16,4096]{1,0:T(8,128)} %bitcast.8, f32[32,128]{1,0:T(8,128)} %bitcast.10), custom_call_target="tpu_custom_call" | custom-call | flops 16777216 | bytes 2097152 | tf_op jit(solution)/shard_map/early/pallas_call | solution.py:396
  18.7 0.7 %constant_dynamic-slice_fusion = (f32[3,128]{1,0:T(4,128)S(1)}, f32[3,128]{1,0:T(4,128)S(1)}) fusion(f32[3,12288]{1,0:T(4,128)} %taps_hbm.3, s32[]{:T(128)S(6)} %select_n.11, s32[]{:T(128)S(6)} %select_n.10), kind=kLoop, calls=%fused_computation.1 | loop fusion | bytes 6152 | tf_op jit(solution)/shard_map/dynamic_slice | solution.py:375
  19.4 0.7 %dynamic-slice_bitcast_fusion.rates_ref = f32[16,128]{1,0:T(8,128)S(1)} fusion(f32[4096,16]{0,1:T(8,128)} %param.7, s32[]{:T(128)S(6)} %select_n.9), kind=kLoop, calls=%fused_computation | loop fusion | bytes 16388 | tf_op jit(solution)/shard_map/dynamic_slice | solution.py:375
  20.1 1.4 %all-to-all-done.got_ref = bf16[32,24,128]{2,1,0:T(8,128)(2,1)S(1)} async-done(((bf16[32,24,128]{2,1,0:T(8,128)(2,1)}), bf16[32,24,128]{2,1,0:T(8,128)(2,1)S(1)}, u32[]{:S(2)}, u32[]{:S(2)}) %all-to-all-start) | async-done | bytes 196640 | tf_op jit(solution)/shard_map/all_to_all | solution.py:365
  21.5 0.9 %scan.1.after_ref = bf16[32,16,128]{2,1,0:T(8,128)(2,1)} custom-call(bf16[32,24,128]{2,1,0:T(8,128)(2,1)S(1)} %all-to-all-done.got_ref, f32[16,128]{1,0:T(8,128)S(1)} %dynamic-slice_bitcast_fusion.rates_ref, f32[3,128]{1,0:T(4,128)S(1)} %get-tuple-element.24.tk_ref, f32[3,128]{1,0:T(4,128)S(1)} %get-tuple-element.23.tv_ref, ...), custom_call_target="tpu_custom_call" | custom-call | tf_op jit(solution)/shard_map/scan/pallas_call | solution.py:416
  22.4 4.4 %all-to-all-start.1 = ((bf16[32,16,128]{2,1,0:T(8,128)(2,1)}), bf16[32,16,128]{2,1,0:T(8,128)(2,1)S(1)}, u32[]{:S(2)}, u32[]{:S(2)}) async-start(bf16[32,16,128]{2,1,0:T(8,128)(2,1)} %scan.1.after_ref), calls=%async_computation.1 | async-start | bytes 262144 | tf_op jit(solution)/shard_map/all_to_all | solution.py:365
  26.8 3.4 %collective-permute-start = (bf16[2,12288]{1,0:T(2,128)(2,1)S(1)}, bf16[2,12288]{1,0:T(2,128)(2,1)S(1)}, u32[]{:S(2)}, u32[]{:S(2)}) collective-permute-start(bf16[2,12288]{1,0:T(2,128)(2,1)S(1)} %get-tuple-element.17), channel_id=1, source_target_pairs={{0,1},{1,2},{2,3},{3,4},{4,5},{5,6},{6,7},{7,8},{8,9},{9,10},{10,1... | collective-permute-start | bytes 147464 | tf_op jit(solution)/shard_map/ppermute | solution.py:414
  30.2 5.6 %collective-permute-done.halo_ref = bf16[2,12288]{1,0:T(2,128)(2,1)S(1)} collective-permute-done((bf16[2,12288]{1,0:T(2,128)(2,1)S(1)}, bf16[2,12288]{1,0:T(2,128)(2,1)S(1)}, u32[]{:S(2)}, u32[]{:S(2)}) %collective-permute-start) | collective-permute-done | bytes 49184 | tf_op jit(solution)/shard_map/ppermute | solution.py:414
  35.8 8.0 %late.1 = (f32[2048,128]{1,0:T(8,128)}, f32[4096,128]{1,0:T(8,128)}, f32[32,16,8,128]{3,2,1,0:T(8,128)}, f32[32,16,128]{2,1,0:T(8,128)}, f32[32,8,128]{2,1,0:T(8,128)}) custom-call(bf16[128,12288]{1,0:T(8,128)(2,1)} %proj_ref.5, bf16[2,12288]{1,0:T(2,128)(2,1)S(1)} %collective-permute-done.halo_ref, bf16[32,16,128]{2,1,0:T(8,128)(2,1)} %scan.1.after_ref, ...), custom_call_target="tpu_custom_call" | custom-call | flops 16777216 | bytes 2097152 | tf_op jit(solution)/shard_map/late/pallas_call | solution.py:432
  43.9 0.0 all-to-all-done.1.carry_ref
  43.9 5.0 %final.1 = bf16[128,4096]{1,0:T(8,128)(2,1)} custom-call(bf16[32,16,128]{2,1,0:T(8,128)(2,1)S(1)} %all-to-all-done.1.carry_ref, f32[2048,128]{1,0:T(8,128)} %get-tuple-element.16.after_ref.early_hbm, f32[2048,128]{1,0:T(8,128)} %get-tuple-element.18.late_hbm, f32[4096,128]{1,0:T(8,128)} %get-tuple-element.19.query_hbm, ...), custom_call_target="tpu_custom_call" | custom-call | tf_op jit(solution)/shard_map/final/pallas_call | solution.py:455
Async XLA Ops:
  6.9 14.6 %all-to-all-start = ((bf16[32,24,128]{2,1,0:T(8,128)(2,1)}), bf16[32,24,128]{2,1,0:T(8,128)(2,1)S(1)}, u32[]{:S(2)}, u32[]{:S(2)}) async-start(bf16[32,24,128]{2,1,0:T(8,128)(2,1)} %get-tuple-element.14), calls=%async_computation | async-start | bytes 393216 | tf_op jit(solution)/shard_map/all_to_all | solution.py:365
  22.4 21.5 %all-to-all-start.1 = ((bf16[32,16,128]{2,1,0:T(8,128)(2,1)}), bf16[32,16,128]{2,1,0:T(8,128)(2,1)S(1)}, u32[]{:S(2)}, u32[]{:S(2)}) async-start(bf16[32,16,128]{2,1,0:T(8,128)(2,1)} %scan.1.after_ref), calls=%async_computation.1 | async-start | bytes 262144 | tf_op jit(solution)/shard_map/all_to_all | solution.py:365
  26.8 9.0 %collective-permute-start = (bf16[2,12288]{1,0:T(2,128)(2,1)S(1)}, bf16[2,12288]{1,0:T(2,128)(2,1)S(1)}, u32[]{:S(2)}, u32[]{:S(2)}) collective-permute-start(bf16[2,12288]{1,0:T(2,128)(2,1)S(1)} %get-tuple-element.17), channel_id=1, source_target_pairs={{0,1},{1,2},{2,3},{3,4},{4,5},{5,6},{6,7},{7,8},{8,9},{9,10},{10,1... | collective-permute-start | bytes 147464 | tf_op jit(solution)/shard_map/ppermute | solution.py:414
